TPU v7x, 128 devices: a whole 4x4x4 slice. The times are simulated.
128 devices in a mesh: prow: 8 (over z, core), pcol: 16 (over x, y).
Axes of the slice: x: 4, y: 4, z: 4, core: 2. Of those that a mesh axis runs over, the one named last changes fastest.
Arguments:
- child_inverse: float32 [8, 16, 8, 256, 256], P('prow', 'pcol'), as said below
- child_rhs: float32 [8, 16, 8, 256, 256], P('prow', 'pcol'), may hold values from -6 to 6
- panels: float32 [8, 16, 8, 128, 256], P('prow', 'pcol'), may hold values from -0.125 to 0.125
- panel_parent: int32 [8, 16, 8, 1], P('prow', 'pcol'), may hold values from 0 to 15; in each aligned block of 8 rows (0 to 7, 8 to 15, ..., all dimensions but the last counted through in order) no two rows name the same one
- panel_rows: int32 [8, 16, 8, 128], P('prow', 'pcol'), may hold values from 0 to 255, as said below
- parent_inverse: float32 [8, 16, 256, 256], P('prow', 'pcol'), as said below
- parent_rhs: float32 [8, 16, 256, 256], P('prow', 'pcol'), may hold values from -6 to 6
Outputs:
- child_solution: float32 [8, 16, 8, 256, 256], P('prow', 'pcol')
- parent_solution: float32 [8, 16, 256, 256], P('prow', 'pcol')
Inputs may be any that keep to these rules, and one draw needn't show every extreme that they name: `panel_parent`: in the 8 slots of one device no parent is named more than 1 times. `panel_rows`: each slot lists 128 different columns of its parent in ascending order. `child_inverse`: lower triangular, with diagonal entries between 0.4 and 2.1. `parent_inverse`: lower triangular, with diagonal entries between 0.4 and 2.1.
All inputs are finite; a program needn't handle non-finite values.
Results may differ from a plain program's by a relative error of at most 0.00005.
Values sent between devices are 32-bit elements; how exact they have to be, the bound alone decides.
A program may use at most 64 MiB of HBM per device.

v0:
```python
import jax
import jax.numpy as jnp
from jax import lax
from jax.sharding import PartitionSpec as P

highest = lax.Precision.HIGHEST


def body(child_inverse, child_rhs, panels, panel_parent, panel_rows, parent_inverse, parent_rhs):
    own_inverse = child_inverse[0, 0]
    own_rhs = child_rhs[0, 0]
    own_panels = panels[0, 0]
    slot_count, row_count, node_width = own_panels.shape
    columns = own_rhs.shape[-1]
    group_cols = lax.axis_size("pcol")
    own_parent = panel_parent[0, 0][:, 0]
    own_rows = panel_rows[0, 0]
    target = (own_parent[:, None] * node_width + own_rows).reshape(-1)
    y_child = jnp.einsum("kab,kbn->kan", own_inverse, own_rhs, precision=highest)
    update = jnp.einsum(
        "sra,san->srn",
        own_panels,
        lax.all_to_all(y_child, "prow", split_axis=0, concat_axis=0, tiled=True),
        precision=highest,
    )
    parent_own = parent_inverse[0, 0]
    initial = jnp.zeros((group_cols * node_width, columns), jnp.float32)
    row_terms = initial.at[target].add(update.reshape(-1, columns))
    parent_sum = lax.psum_scatter(row_terms, "pcol", scatter_dimension=0, tiled=True)
    y_parent = jnp.dot(parent_own, parent_rhs[0, 0] - parent_sum, precision=highest)
    parent_solution = jnp.dot(parent_own.T, y_parent, precision=highest)
    everyone = lax.all_gather(parent_solution, "pcol", axis=0, tiled=True)
    picked = everyone[target].reshape(slot_count, row_count, columns)
    correction = jnp.einsum("sra,srn->san", own_panels, picked, precision=highest)
    returned = lax.all_to_all(correction, "prow", split_axis=0, concat_axis=0, tiled=True)
    child_solution = jnp.einsum("kba,kbn->kan", own_inverse, y_child - returned, precision=highest)
    return (child_solution[None, None], parent_solution[None, None])


def solution(mesh):
    placed = (
        P("prow", "pcol", None, None, None),
        P("prow", "pcol", None, None, None),
        P("prow", "pcol", None, None, None),
        P("prow", "pcol", None, None),
        P("prow", "pcol", None, None),
        P("prow", "pcol", None, None),
        P("prow", "pcol", None, None),
    )
    return jax.shard_map(
        body,
        mesh=mesh,
        in_specs=placed,
        out_specs=(P("prow", "pcol", None, None, None), P("prow", "pcol", None, None)),
        check_vma=False,
    )
```

profile of v0, /device:TPU:1, one launch (start us, length us, event | category | flops | bytes accessed | tf_op | source)
XLA Modules:
  0.0 261.1 jit_solution(9404664532170016938)
XLA Ops:
  7.2 0.0 copy-start
  7.2 1.6 copy-done
  8.8 5.0 %fusion = f32[8,256,256]{2,1,0:T(8,128)} fusion(f32[1,1,8,256,256]{4,3,2,1,0:T(8,128)} %param.8, f32[1,1,8,256,256]{4,3,2,1,0:T(8,128)S(1)} %copy-done), kind=kOutput, calls=%fused_computation.2 | convolution fusion | flops 1610612736 | bytes 6291456 | tf_op jit(solution)/shard_map/kab,kbn->kan/dot_general | solution.py:19
  13.8 6.9 %all-to-all-start = ((f32[8,256,256]{2,1,0:T(8,128)}), f32[8,256,256]{2,1,0:T(8,128)}, u32[]{:S(2)}, u32[]{:S(2)}) async-start(f32[8,256,256]{2,1,0:T(8,128)} %fusion), calls=%async_computation | async-start | bytes 4194304 | tf_op jit(solution)/shard_map/all_to_all | solution.py:23
  20.7 0.0 reduce-scatter.2.cloned.1.call-start
  20.7 0.1 add.33
  20.8 26.3 %all-to-all-done = f32[8,256,256]{2,1,0:T(8,128)} async-done(((f32[8,256,256]{2,1,0:T(8,128)}), f32[8,256,256]{2,1,0:T(8,128)}, u32[]{:S(2)}, u32[]{:S(2)}) %all-to-all-start) | async-done | bytes 2097184 | tf_op jit(solution)/shard_map/all_to_all | solution.py:23
  47.2 3.9 %fusion.14 = f32[8,256,128]{1,2,0:T(8,128)} fusion(f32[8,256,256]{2,1,0:T(8,128)} %all-to-all-done, f32[1,1,8,128,256]{4,3,2,1,0:T(8,128)S(1)} %copy-done.1), kind=kOutput, calls=%fused_computation.13 | convolution fusion | flops 805306368 | bytes 4194304 | tf_op jit(solution)/shard_map/sra,san->srn/dot_general | solution.py:20
  51.1 8.7 %scatter_custom_fusion = f32[4096,256]{1,0:T(8,128)} fusion(s32[1024]{0:T(1024)S(1)} %bitcast.48, f32[1024,256]{1,0:T(8,128)} %bitcast.47, f32[]{:T(128)} %constant.0.clone.1), kind=kCustom, calls=%fused_computation.8 | custom fusion | flops 262144 | bytes 4194816 | tf_op jit(solution)/shard_map/scatter-add | solution.py:28
  59.8 0.0 reduce-scatter.2.cloned.1.call-update
  59.8 0.0 all-gather.2.cloned.1.call-start
  59.9 75.7 %reduce-scatter.2.cloned.1.call-done = f32[256,256]{1,0:T(8,128)} async-done(((f32[4096,256]{1,0:T(8,128)}), f32[256,256]{1,0:T(8,128)}) %reduce-scatter.2.cloned.1.call-update) | async-done | bytes 262160 | tf_op jit(solution)/shard_map/reduce_scatter | solution.py:29
  135.6 1.5 fusion.18
  137.1 1.1 fusion.16
  138.2 0.0 all-gather.2.cloned.1.call-update
  138.2 57.9 %all-gather.2.cloned.1.call-done = f32[4096,256]{0,1:T(8,128)} async-done(((f32[256,256]{0,1:T(8,128)}), f32[4096,256]{0,1:T(8,128)}) %all-gather.2.cloned.1.call-update) | async-done | bytes 4194320 | tf_op jit(solution)/shard_map/all_gather | solution.py:32
  196.1 5.6 %copy.9 = f32[4096,256]{1,0:T(8,128)} copy(f32[4096,256]{0,1:T(8,128)} %all-gather.2.cloned.1.call-done) | data formatting | bytes 8388608 | tf_op jit(solution)/shard_map/all_gather | solution.py:32
  201.7 5.6 %gather_fusion = f32[1024,256]{1,0:T(8,128)S(1)} fusion(f32[4096,256]{1,0:T(8,128)} %copy.9, s32[1024]{0:T(1024)S(1)} %broadcast_clamp_fusion), kind=kCustom, calls=%fused_computation | custom fusion | bytes 2101248 | tf_op jit(solution)/shard_map/gather | solution.py:33
  207.4 4.4 %convolution_bitcast_fusion = f32[8,256,256]{2,1,0:T(8,128)} fusion(f32[8,128,256]{2,1,0:T(8,128)S(1)} %bitcast.44, f32[1,1,8,128,256]{4,3,2,1,0:T(8,128)} %param.9), kind=kOutput, calls=%fused_computation.11 | convolution fusion | flops 805306368 | bytes 4194304 | tf_op jit(solution)/shard_map/sra,srn->san/dot_general | solution.py:34
  211.8 6.1 %all-to-all-start.1 = ((f32[8,256,256]{2,1,0:T(8,128)}), f32[8,256,256]{2,1,0:T(8,128)}, u32[]{:S(2)}, u32[]{:S(2)}) async-start(f32[8,256,256]{2,1,0:T(8,128)} %convolution_bitcast_fusion), calls=%async_computation.2 | async-start | bytes 4194304 | tf_op jit(solution)/shard_map/all_to_all | solution.py:35
  217.8 0.8 copy.12
  218.7 25.6 %all-to-all-done.1 = f32[8,256,256]{2,1,0:T(8,128)} async-done(((f32[8,256,256]{2,1,0:T(8,128)}), f32[8,256,256]{2,1,0:T(8,128)}, u32[]{:S(2)}, u32[]{:S(2)}) %all-to-all-start.1) | async-done | bytes 2097184 | tf_op jit(solution)/shard_map/all_to_all | solution.py:35
  244.3 7.1 %fusion.8 = f32[1,1,8,256,256]{3,4,2,1,0:T(8,128)} fusion(f32[1,1,8,256,256]{4,3,2,1,0:T(8,128)S(1)} %copy-done, f32[8,256,256]{2,1,0:T(8,128)} %fusion, f32[8,256,256]{2,1,0:T(8,128)} %all-to-all-done.1), kind=kOutput, calls=%fused_computation.10 | convolution fusion | flops 1611137024 | bytes 8388608 | tf_op jit(solution)/shard_map/kba,kbn->kan/dot_general | solution.py:36
  251.3 2.9 %copy.11 = f32[1,1,8,256,256]{4,3,2,1,0:T(8,128)} copy(f32[1,1,8,256,256]{3,4,2,1,0:T(8,128)} %fusion.8) | data formatting | bytes 4194304
  (15 shorter events, 0.0 us)
Async XLA Ops:
  7.2 1.6 copy-start
  13.8 7.0 %copy-start.6 = (s32[1,1,8,1]{2,3,1,0:T(1,128)S(1)}, s32[1,1,8,1]{2,3,1,0:T(1,128)}, u32[]{:S(2)}) copy-start(s32[1,1,8,1]{2,3,1,0:T(1,128)} %param.10) | copy-start | bytes 100
  13.8 7.0 %copy-start.5 = (s32[1,1,8,128]{3,2,1,0:T(8,128)S(1)}, s32[1,1,8,128]{3,2,1,0:T(8,128)}, u32[]{:S(2)}) copy-start(s32[1,1,8,128]{3,2,1,0:T(8,128)} %param.11) | copy-start | bytes 12292
  13.8 33.4 %copy-start.1 = (f32[1,1,8,128,256]{4,3,2,1,0:T(8,128)S(1)}, f32[1,1,8,128,256]{4,3,2,1,0:T(8,128)}, u32[]{:S(2)}) copy-start(f32[1,1,8,128,256]{4,3,2,1,0:T(8,128)} %param.9) | copy-start | bytes 3145732
  13.8 33.4 %all-to-all-start = ((f32[8,256,256]{2,1,0:T(8,128)}), f32[8,256,256]{2,1,0:T(8,128)}, u32[]{:S(2)}, u32[]{:S(2)}) async-start(f32[8,256,256]{2,1,0:T(8,128)} %fusion), calls=%async_computation | async-start | bytes 4194304 | tf_op jit(solution)/shard_map/all_to_all | solution.py:23
  20.7 114.8 %reduce-scatter.2.cloned.1.call-start = ((), (), s32[]{:S(2)}) async-start(), calls=%async_computation.3 | async-start | bytes 4456448 | tf_op jit(solution)/shard_map/reduce_scatter | solution.py:29
  59.8 75.7 %copy-start.3 = (f32[1,1,256,256]{3,2,1,0:T(8,128)S(1)}, f32[1,1,256,256]{3,2,1,0:T(8,128)}, u32[]{:S(2)}) copy-start(f32[1,1,256,256]{3,2,1,0:T(8,128)} %param.12) | copy-start | bytes 786436
  59.8 75.7 %copy-start.4 = (f32[1,1,256,256]{3,2,1,0:T(8,128)S(1)}, f32[1,1,256,256]{3,2,1,0:T(8,128)}, u32[]{:S(2)}) copy-start(f32[1,1,256,256]{3,2,1,0:T(8,128)} %param.13) | copy-start | bytes 786436
  59.8 136.2 %all-gather.2.cloned.1.call-start = ((), (), s32[]{:S(2)}) async-start(), calls=%async_computation.4 | async-start | bytes 4456448 | tf_op jit(solution)/shard_map/all_gather | solution.py:32
  211.7 6.1 %copy-start.2 = (f32[256,256]{1,0:T(8,128)S(1)}, f32[256,256]{1,0:T(8,128)}, u32[]{:S(2)}) copy-start(f32[256,256]{1,0:T(8,128)} %fusion.16) | copy-start | bytes 786436
  211.8 32.5 %all-to-all-start.1 = ((f32[8,256,256]{2,1,0:T(8,128)}), f32[8,256,256]{2,1,0:T(8,128)}, u32[]{:S(2)}, u32[]{:S(2)}) async-start(f32[8,256,256]{2,1,0:T(8,128)} %convolution_bitcast_fusion), calls=%async_computation.2 | async-start | bytes 4194304 | tf_op jit(solution)/shard_map/all_to_all | solution.py:35
Sparse Core Ops, SparseCore 0:
  60.0 75.5 reduce-scatter.1
  138.4 57.5 all-gather.1
where the time goes:
time: 262 us; the launch traced here: 261 us
  waiting for transfers between devices  185 us (71%)
  matrix products  23 us (9%)
  local copies, waits for them, and re-layouts  16.7 us (6%)
  between operations  14.1 us (5%)
  starting transfers between devices  13.1 us (5%)
  other arithmetic  8.72 us (3%)
    reduce_scatter x1, waiting for transfers between devices, body(): lax.psum_scatter(row_terms, 'pcol', scatter_dimension=0, tiled=True)  75.7 us
    all_gather x1, waiting for transfers between devices, body(): everyone = lax.all_gather(parent_solution, 'pcol', axis=0, tiled=True)  57.9 us
    all_to_all x1, waiting for transfers between devices, body(): lax.all_to_all(y_child, 'prow', split_axis=0, concat_axis=0, tiled=True)  26.3 us
    all_to_all x1, waiting for transfers between devices, body(): lax.all_to_all(correction, 'prow', split_axis=0, concat_axis=0, tiled=True)  25.6 us
    scatter-add x1, other arithmetic, body(): row_terms = initial.at[target].add(update.reshape(-1, columns))  8.7 us
    dot_general x1, matrix products, body(): jnp.einsum('kba,kbn->kan', own_inverse, y_child - returned, precision=hig...  7.05 us
    all_to_all x1, starting transfers between devices, body(): lax.all_to_all(y_child, 'prow', split_axis=0, concat_axis=0, tiled=True)  6.95 us
    all_to_all x1, starting transfers between devices, body(): lax.all_to_all(correction, 'prow', split_axis=0, concat_axis=0, tiled=True)  6.1 us
  transfers between devices with their start and end apart: 4, of which 4 were waited for; matrix products, arithmetic and copies ran while one was open for 0% of the time, Pallas kernels for 0%

commit v1 on v0

v1 whole, which is shorter than its diff:
```python
import jax
import jax.numpy as jnp
from jax import lax
from jax.experimental import pallas as pl
from jax.experimental.pallas import tpu as pltpu
from jax.sharding import PartitionSpec as P

MESH = pl.DeviceIdType.MESH
F32 = jnp.float32
BF16 = jnp.bfloat16
W = 256
R = 128
CH = 8
C = 2
CW = 128
DMA = pltpu.SemaphoreType.DMA


def split(value):
    high = value.astype(BF16)
    low = (value - high.astype(F32)).astype(BF16)
    return high, low


def dot(a, b, dims=((1,), (0,))):
    return lax.dot_general(a, b, (dims, ((), ())), preferred_element_type=F32)


def product(a, b, dims=((1,), (0,))):
    a_high, a_low = split(a)
    b_high, b_low = split(b)
    return dot(a_high, b_high, dims) + (dot(a_high, b_low, dims) + dot(a_low, b_high, dims))


def chosen(one_hot, b):
    b_high, b_low = split(b)
    return dot(one_hot, b_high) + dot(one_hot, b_low)


def kernel(
    parent_ids, inverse_hbm, rhs_hbm, panels_hbm, rows_ref, pinv_ref, prhs_ref,
    child_out, parent_out,
    inverse, rhs, panels, y_send, y_in, update, rows_send, rows_in, one_hot, one_hot_t,
    first_send, first_in, dense, second_in, k_high, k_low, z_parent, x_block, pick_send, pick_in_0, pick_in_1,
    v_send, v_in, panel_in, gain_high, gain_low, z_child, out_buf,
    load_sem, out_sem, y_s, y_r, p_s, p_r, i_s, i_r, s1_s, s1_r, s2_s, s2_r, t1_s, t1_r, t2_s, t2_r, v_s, v_r,
):
    r = lax.axis_index("prow")
    q = lax.axis_index("pcol")
    core = r % 2
    x, y = q // 4, q % 4
    cls = (x + y + core) % 2
    own_pos = jnp.where(cls == 0, y, x)
    other_pos = jnp.where(cls == 0, x, y)
    t_self = own_pos // 2
    first_pos = (x, y)
    pick_in = (pick_in_0, pick_in_1)

    def first_dev(f, a):
        return (r, a * 4 + y) if f == 0 else (r, x * 4 + a)

    def own_dev(a):
        return (r, jnp.where(cls == 0, x * 4 + a, a * 4 + y))

    def other_dev(a):
        return (r, jnp.where(cls == 0, a * 4 + y, x * 4 + a))

    def remote(src, dst, send, recv, dev):
        return pltpu.make_async_remote_copy(
            src_ref=src, dst_ref=dst, send_sem=send, recv_sem=recv, device_id=dev, device_id_type=MESH
        )

    barrier = pltpu.get_barrier_semaphore()

    def greet(j, carry):
        pl.semaphore_signal(barrier, inc=1, device_id=((r + j) % 8, q), device_id_type=MESH)
        return carry

    lax.fori_loop(1, 8, greet, 0)
    for f in range(2):
        for d in range(1, 4):
            pl.semaphore_signal(barrier, inc=1, device_id=first_dev(f, (first_pos[f] + d) % 4), device_id_type=MESH)

    def load(k):
        return (
            pltpu.make_async_copy(inverse_hbm.at[k], inverse.at[k], load_sem.at[0, k]),
            pltpu.make_async_copy(rhs_hbm.at[k], rhs.at[k], load_sem.at[1, k]),
        )

    def start_load(j, carry):
        for copy in load((r + 1 + j) % 8):
            copy.start()
        return carry

    lax.fori_loop(0, 8, start_load, 0)
    panel_load = pltpu.make_async_copy(panels_hbm, panels, load_sem.at[2, 0])
    panel_load.start()

    def y_copy(c, k):
        return remote(y_send.at[c, k], y_in.at[c, r], y_s.at[c, k], y_r.at[c, r], (k, q))

    def y_wait(c, s):
        return remote(y_send.at[c, s], y_in.at[c, s], y_s.at[c, s], y_r.at[c, s], (s, q))

    def forward(k):
        for copy in load(k):
            copy.wait()
        value = product(inverse[k], rhs[k])
        for c in range(C):
            y_send[c, k] = value[:, c * CW:(c + 1) * CW]

    forward((r + 1) % 8)
    pl.semaphore_wait(barrier, 13)
    y_copy(0, (r + 1) % 8).start()

    def forward_step(j, carry):
        k = (r + j) % 8
        forward(k)
        y_copy(0, k).start()
        return carry

    lax.fori_loop(2, 8, forward_step, 0)
    forward(r)
    for c in range(C):
        y_in[c, r] = y_send[c, r]

    def parent_of(f, a, t):
        if f == 0:
            return a * 4 + (a + core) % 2 + 2 * t
        return ((a + core + 1) % 2 + 2 * t) * 4 + a

    def rows_copy(f, a):
        return remote(rows_send.at[f, a], rows_in.at[f, first_pos[f]], i_s.at[f, a], i_r.at[f, first_pos[f]], first_dev(f, a))

    def rows_wait(f, a):
        return remote(rows_send.at[f, a], rows_in.at[f, a], i_s.at[f, a], i_r.at[f, a], first_dev(f, a))

    for f in range(2):
        for a in range(4):
            for t in range(2):
                p = parent_of(f, a, t)
                listed = jnp.full((1, R), -1, jnp.int32)
                for s in range(CH):
                    listed = jnp.where(parent_ids[s] == p, rows_ref[s:s + 1, :], listed)
                rows_send[f, a, t:t + 1, :] = listed
            rows_send[f, a, 2:8, :] = jnp.zeros((6, R), jnp.int32)
        rows_in[f, first_pos[f]] = rows_send[f, first_pos[f]]
        for d in range(1, 4):
            rows_copy(f, (first_pos[f] + d) % 4).start()

    def y_next(j, carry):
        k = (r + j) % 8
        y_copy(0, k).wait_send()
        y_copy(1, k).start()
        return carry

    lax.fori_loop(1, 8, y_next, 0)

    gram = product(pinv_ref[...], pinv_ref[...], ((0,), (0,)))
    high, low = split(gram)
    k_high[...] = high
    k_low[...] = low
    value = product(gram, prhs_ref[...])
    for c in range(C):
        z_parent[c] = value[:, c * CW:(c + 1) * CW]

    for f in range(2):
        for d in range(1, 4):
            rows_wait(f, (first_pos[f] + d) % 4).wait_recv()
        for a in range(4):
            for t in range(2):
                listed = rows_in[f, a, t:t + 1, :]
                places = lax.broadcasted_iota(jnp.int32, (W, R), 0)
                matrix = jnp.where(places == listed, 1.0, 0.0).astype(F32)
                one_hot[f, t, :, a * R:(a + 1) * R] = matrix.astype(BF16)
                one_hot_t[f, t, a * R:(a + 1) * R, :] = matrix.T.astype(BF16)
    panel_load.wait()

    def first_copy(c, f, a):
        return remote(first_send.at[c, f, a], first_in.at[c, f, first_pos[f]], s1_s.at[c, f, a], s1_r.at[c, f, first_pos[f]], first_dev(f, a))

    def first_wait(c, f, a):
        return remote(first_send.at[c, f, a], first_in.at[c, f, a], s1_s.at[c, f, a], s1_r.at[c, f, a], first_dev(f, a))

    def step_update(c):
        def one(j, carry):
            s = (r + j) % 8
            y_wait(c, s).wait_recv()
            update[c, s] = product(panels[s], y_in[c, s])
            return carry

        update[c, r] = product(panels[r], y_in[c, r])
        lax.fori_loop(1, 8, one, 0)
        for f in range(2):
            for a in range(4):
                for t in range(2):
                    p = parent_of(f, a, t)
                    slot = jnp.int32(0)
                    for s in range(1, CH):
                        slot = jnp.where(parent_ids[s] == p, s, slot)
                    first_send[c, f, a, t] = update[c, slot]
            first_in[c, f, first_pos[f]] = first_send[c, f, first_pos[f]]
            for d in (2, 1, 3):
                first_copy(c, f, (first_pos[f] + d) % 4).start()

    def second_own(c):
        a = (own_pos + 2) % 4
        return remote(dense.at[c, cls, 1 - t_self], second_in.at[c, own_pos], s2_s.at[c, 2], s2_r.at[c, own_pos], own_dev(a))

    def second_other(c, t):
        a = (other_pos + 1) % 2 + 2 * t
        return remote(dense.at[c, 1 - cls, t], second_in.at[c, other_pos], s2_s.at[c, t], s2_r.at[c, other_pos], other_dev(a))

    def second_wait(c, a):
        return remote(dense.at[c, 0, 0], second_in.at[c, a], s2_s.at[c, 0], s2_r.at[c, a], own_dev(a))

    def step_dense(c):
        for f in range(2):
            for d in (1, 3, 2):
                first_wait(c, f, (first_pos[f] + d) % 4).wait_recv()
            for t in range(2):
                blocks = first_in[c, f, :, t].reshape(4 * R, CW)
                dense[c, f, t] = chosen(one_hot[f, t], blocks)
        second_own(c).start()
        for t in range(2):
            second_other(c, t).start()

    def x_copy(c, d):
        return remote(x_block.at[c, cls, t_self], x_block.at[c, cls, t_self], t1_s.at[c, d], t1_r.at[c, cls, t_self], own_dev((own_pos + d) % 4))

    def x_wait_own(c):
        return remote(x_block.at[c, cls, 1 - t_self], x_block.at[c, cls, 1 - t_self], t1_s.at[c, 1], t1_r.at[c, cls, 1 - t_self], own_dev((own_pos + 2) % 4))

    def x_wait_other(c, t):
        a = (other_pos + 1) % 2 + 2 * t
        return remote(x_block.at[c, 1 - cls, t], x_block.at[c, 1 - cls, t], t1_s.at[c, 1], t1_r.at[c, 1 - cls, t], other_dev(a))

    def step_parent(c):
        total = dense[c, cls, t_self]
        for d in (1, 3, 2):
            a = (own_pos + d) % 4
            second_wait(c, a).wait_recv()
            total = total + second_in[c, a]
        high, low = split(total)
        k_h = k_high[...]
        solution_block = z_parent[c] - (dot(k_h, high) + (dot(k_h, low) + dot(k_low[...], high)))
        x_block[c, cls, t_self] = solution_block
        for d in (2, 1, 3):
            x_copy(c, d).start()
        parent_out[:, c * CW:(c + 1) * CW] = solution_block

    def pick_copy(c, f, a):
        return remote(pick_send.at[c, f, a], pick_in[c].at[f, first_pos[f]], t2_s.at[c, f, a], t2_r.at[c, f, first_pos[f]], first_dev(f, a))

    def pick_wait(c, f, a):
        return remote(pick_send.at[c, f, a], pick_in[c].at[f, a], t2_s.at[c, f, a], t2_r.at[c, f, a], first_dev(f, a))

    def step_pick(c):
        for t in range(2):
            x_wait_other(c, t).wait_recv()
        x_wait_own(c).wait_recv()
        for f in range(2):
            for t in range(2):
                picked = chosen(one_hot_t[f, t], x_block[c, f, t])
                pick_send[c, f, :, t] = picked.reshape(4, R, CW)
            pick_in[c][f, first_pos[f]] = pick_send[c, f, first_pos[f]]
            for d in (2, 1, 3):
                pick_copy(c, f, (first_pos[f] + d) % 4).start()

    def v_copy(c, s):
        return remote(v_send.at[c, s], v_in.at[c, r], v_s.at[c, s], v_r.at[c, r], (s, q))

    def v_wait(c, s):
        return remote(v_send.at[c, s], v_in.at[c, s], v_s.at[c, s], v_r.at[c, s], (s, q))

    def step_return(c):
        for f in range(2):
            for d in (1, 3, 2):
                pick_wait(c, f, (first_pos[f] + d) % 4).wait_recv()

        def one(j, carry):
            s = (r + j) % 8
            p = parent_ids[s]
            x_p, y_p = p // 4, p % 4
            f = (x_p + y_p + core) % 2
            a = jnp.where(f == 0, x_p, y_p)
            t = jnp.where(f == 0, y_p, x_p) // 2
            v_send[c, s] = pick_in[c][f, a, t]
            return carry

        lax.fori_loop(0, 8, one, 0)

        def begin(j, carry):
            v_copy(c, (r + j) % 8).start()
            return carry

        lax.fori_loop(1, 8, begin, 0)
        v_in[c, r] = v_send[c, r]

    def panel_copy(k):
        return remote(panels.at[k], panel_in.at[r], p_s.at[k], p_r.at[r], (k, q))

    def panel_wait(s):
        return remote(panels.at[s], panel_in.at[s], p_s.at[s], p_r.at[s], (s, q))

    def send_panels():
        def one(j, carry):
            k = (r + j) % 8
            y_copy(1, k).wait_send()
            panel_copy(k).start()
            return carry

        lax.fori_loop(1, 8, one, 0)
        panel_in[r] = panels[r]

    def gains():
        def one(j, carry):
            s = (r + j) % 8

            @pl.when(j > 0)
            def _():
                panel_wait(s).wait_recv()

            high, low = split(product(panel_in[s], inverse[s]).T)
            gain_high[s] = high
            gain_low[s] = low
            return carry

        lax.fori_loop(0, 8, one, 0)

    def solved():
        def one(k, carry):
            i_high, i_low = split(inverse[k].T)
            for c in range(C):
                y_high, y_low = split(y_send[c, k])
                z_child[c, k] = dot(i_high, y_high) + (dot(i_high, y_low) + dot(i_low, y_high))
            return carry

        lax.fori_loop(0, 8, one, 0)

    def out_copy(c, k):
        return pltpu.make_async_copy(out_buf.at[k, :, pl.ds(c * CW, CW)], child_out.at[k, :, pl.ds(c * CW, CW)], out_sem.at[c, k])

    def step_final(c):
        def one(j, carry):
            s = (r + j) % 8

            @pl.when(j > 0)
            def _():
                v_wait(c, s).wait_recv()

            high, low = split(v_in[c, s])
            g_high = gain_high[s]
            value = z_child[c, s] - (dot(g_high, high) + (dot(g_high, low) + dot(gain_low[s], high)))
            out_buf[s, :, c * CW:(c + 1) * CW] = value
            out_copy(c, s).start()
            return carry

        lax.fori_loop(0, 8, one, 0)

    step_update(0)
    solved()
    step_dense(0)
    step_parent(0)
    send_panels()
    step_update(1)
    step_pick(0)
    step_dense(1)
    step_parent(1)
    step_return(0)
    step_pick(1)
    gains()
    step_return(1)
    step_final(0)
    step_final(1)

    def z_done(j, carry):
        k = (r + j) % 8
        panel_copy(k).wait_send()
        for c in range(C):
            v_copy(c, k).wait_send()
        return carry

    lax.fori_loop(1, 8, z_done, 0)
    for f in range(2):
        for d in range(1, 4):
            a = (first_pos[f] + d) % 4
            rows_copy(f, a).wait_send()
            for c in range(C):
                first_copy(c, f, a).wait_send()
                pick_copy(c, f, a).wait_send()
    for c in range(C):
        second_own(c).wait_send()
        for t in range(2):
            second_other(c, t).wait_send()
        for d in range(1, 4):
            x_copy(c, d).wait_send()

    def out_done(k, carry):
        for c in range(C):
            out_copy(c, k).wait()
        return carry

    lax.fori_loop(0, 8, out_done, 0)


def body(child_inverse, child_rhs, panels, panel_parent, panel_rows, parent_inverse, parent_rhs):
    vmem = pl.BlockSpec(memory_space=pltpu.VMEM)
    anywhere = pl.BlockSpec(memory_space=pl.ANY)
    child, parent = pl.pallas_call(
        kernel,
        out_shape=(jax.ShapeDtypeStruct((CH, W, W), F32), jax.ShapeDtypeStruct((W, W), F32)),
        in_specs=[pl.BlockSpec(memory_space=pltpu.SMEM), anywhere, anywhere, anywhere, vmem, vmem, vmem],
        out_specs=(anywhere, vmem),
        scratch_shapes=[
            pltpu.VMEM((CH, W, W), F32),
            pltpu.VMEM((CH, W, W), F32),
            pltpu.VMEM((CH, R, W), F32),
            pltpu.VMEM((C, CH, W, CW), F32),
            pltpu.VMEM((C, CH, W, CW), F32),
            pltpu.VMEM((C, CH, R, CW), F32),
            pltpu.VMEM((2, 4, 8, R), jnp.int32),
            pltpu.VMEM((2, 4, 8, R), jnp.int32),
            pltpu.VMEM((2, 2, W, 4 * R), BF16),
            pltpu.VMEM((2, 2, 4 * R, W), BF16),
            pltpu.VMEM((C, 2, 4, 2, R, CW), F32),
            pltpu.VMEM((C, 2, 4, 2, R, CW), F32),
            pltpu.VMEM((C, 2, 2, W, CW), F32),
            pltpu.VMEM((C, 4, W, CW), F32),
            pltpu.VMEM((W, W), BF16),
            pltpu.VMEM((W, W), BF16),
            pltpu.VMEM((C, W, CW), F32),
            pltpu.VMEM((C, 2, 2, W, CW), F32),
            pltpu.VMEM((C, 2, 4, 2, R, CW), F32),
            pltpu.VMEM((2, 4, 2, R, CW), F32),
            pltpu.VMEM((2, 4, 2, R, CW), F32),
            pltpu.VMEM((C, CH, R, CW), F32),
            pltpu.VMEM((C, CH, R, CW), F32),
            pltpu.VMEM((CH, R, W), F32),
            pltpu.VMEM((CH, W, R), BF16),
            pltpu.VMEM((CH, W, R), BF16),
            pltpu.VMEM((C, CH, W, CW), F32),
            pltpu.VMEM((CH, W, W), F32),
            DMA((3, CH)),
            DMA((C, CH)),
            DMA((C, CH)), DMA((C, CH)),
            DMA((CH,)), DMA((CH,)),
            DMA((2, 4)), DMA((2, 4)),
            DMA((C, 2, 4)), DMA((C, 2, 4)),
            DMA((C, 3)), DMA((C, 4)),
            DMA((C, 4)), DMA((C, 2, 2)),
            DMA((C, 2, 4)), DMA((C, 2, 4)),
            DMA((C, CH)), DMA((C, CH)),
        ],
        compiler_params=pltpu.CompilerParams(collective_id=0, has_side_effects=True, vmem_limit_bytes=56 << 20),
        cost_estimate=pl.CostEstimate(flops=2 * 1300 * 10**6, bytes_accessed=8 << 20, transcendentals=0),
    )(
        panel_parent.reshape(CH), child_inverse[0, 0], child_rhs[0, 0], panels[0, 0], panel_rows[0, 0],
        parent_inverse[0, 0], parent_rhs[0, 0],
    )
    return child[None, None], parent[None, None]


def solution(mesh):
    placed = (
        P("prow", "pcol", None, None, None),
        P("prow", "pcol", None, None, None),
        P("prow", "pcol", None, None, None),
        P("prow", "pcol", None, None),
        P("prow", "pcol", None, None),
        P("prow", "pcol", None, None),
        P("prow", "pcol", None, None),
    )
    return jax.shard_map(
        body,
        mesh=mesh,
        in_specs=placed,
        out_specs=(P("prow", "pcol", None, None, None), P("prow", "pcol", None, None)),
        check_vma=False,
    )
```

time: 262 us -> 89.2 us (0.34)
  waiting for transfers between devices: 185 us -> 0 us
  Pallas kernels: 0 us -> 84.6 us
  matrix products: 23 us -> 0 us
  between operations: 14.1 us -> 0.65 us
  starting transfers between devices: 13.1 us -> 0 us
  local copies, waits for them, and re-layouts: 16.7 us -> 3.79 us
  other arithmetic: 8.72 us -> 0 us
    pallas_call x0 -> x1, Pallas kernels: none -> 84.6 us  [body(): pl.pallas_call(kernel, out_shape=(jax.ShapeDtypeStruct((CH, W, W), F32),...]
    reduce_scatter x1 -> x0, waiting for transfers between devices: 75.7 us -> none  [body(): lax.psum_scatter(row_terms, 'pcol', scatter_dimension=0, tiled=True)]
    all_gather x1 -> x0, waiting for transfers between devices: 57.9 us -> none  [body(): everyone = lax.all_gather(parent_solution, 'pcol', axis=0, tiled=True)]
    all_to_all x2 -> x0, waiting for transfers between devices: 51.9 us -> none  [the longest x1 26.3 us: body(): lax.all_to_all(y_child, 'prow', split_axis=0, concat_axis=0, tiled=True)]
    dot_general x6 -> x0, matrix products: 23 us -> none  [the longest x1 7.05 us: body(): jnp.einsum('kba,kbn->kan', own_inverse, y_child - returned, precision=hig...]
    all_to_all x2 -> x0, starting transfers between devices: 13 us -> none  [the longest x1 6.95 us: body(): lax.all_to_all(y_child, 'prow', split_axis=0, concat_axis=0, tiled=True)]
    scatter-add x1 -> x0, other arithmetic: 8.7 us -> none  [body(): row_terms = initial.at[target].add(update.reshape(-1, columns))]
    gather x1 -> x0, local copies, waits for them, and re-layouts: 5.65 us -> none  [body(): picked = everyone[target].reshape(slot_count, row_count, columns)]
  transfers between devices with their start and end apart: 4 -> 0, of which waited for: 4 -> 0; matrix products, arithmetic and copies ran while one was open for 0% -> 0% of each run, Pallas kernels for 0% -> 0%
where the time goes in v1:
time: 89.2 us; the launch traced here: 89.1 us
  Pallas kernels  84.6 us (95%)
  local copies, waits for them, and re-layouts  3.79 us (4%)
    pallas_call x1, Pallas kernels, body(): pl.pallas_call(kernel, out_shape=(jax.ShapeDtypeStruct((CH, W, W), F32),...  84.6 us
    unnamed x4, local copies, waits for them, and re-layouts  3.79 us

profile of v1, /device:TPU:1, one launch (start us, length us, event | category | flops | bytes accessed | tf_op | source)
XLA Modules:
  0.0 89.1 jit_solution(15940797209653964379)
XLA Ops:
  0.6 84.6 %shard_map.86 = (f32[8,256,256]{2,1,0:T(8,128)}, f32[256,256]{1,0:T(8,128)}) custom-call(s32[8]{0:T(128)} %bitcast.17, f32[8,256,256]{2,1,0:T(8,128)} %bitcast.11, f32[8,256,256]{2,1,0:T(8,128)} %bitcast.12, f32[8,128,256]{2,1,0:T(8,128)} %bitcast.13, s32[8,128]{1,0:T(8,128)} %bitcast.16, f32[256,256]{1,0:T(8,128)} %bitcast.14, f32[256,256]{1,0:T(8,128)} %bitcast.15), custom_call_target="tpu_custom_call" | custom-call | flops 2600000000 | bytes 8388608 | tf_op jit(solution)/shard_map/pallas_call | solution.py:410
  85.3 0.0 copy-start
  85.3 3.1 %copy.11 = f32[1,1,8,256,256]{4,3,2,1,0:T(8,128)} copy(f32[1,1,8,256,256]{4,3,2,1,0:T(8,128)} %bitcast.9) | data formatting | bytes 4194304
  88.4 0.0 copy-done
  88.4 0.7 copy.12
Async XLA Ops:
  85.3 3.1 %copy-start = (f32[256,256]{1,0:T(8,128)S(1)}, f32[256,256]{1,0:T(8,128)}, u32[]{:S(2)}) copy-start(f32[256,256]{1,0:T(8,128)} %get-tuple-element.5) | copy-start | bytes 786436

commit v2 on v1

v2 whole, which is shorter than its diff:
```python
import jax
import jax.numpy as jnp
from jax import lax
from jax.experimental import pallas as pl
from jax.experimental.pallas import tpu as pltpu
from jax.sharding import PartitionSpec as P

MESH = pl.DeviceIdType.MESH
F32 = jnp.float32
BF16 = jnp.bfloat16
DMA = pltpu.SemaphoreType.DMA
W = 256
R = 128
CH = 8
C = 4
CW = 64

SCRATCH = dict(
    inverse=pltpu.VMEM((CH, W, W), F32),
    rhs=pltpu.VMEM((CH, W, W), F32),
    panels=pltpu.VMEM((CH, R, W), F32),
    panel_high=pltpu.VMEM((CH, R, W), BF16),
    panel_low=pltpu.VMEM((CH, R, W), BF16),
    y_send=pltpu.VMEM((C, CH, CW, W), F32),
    y_in=pltpu.VMEM((C, CH, CW, W), F32),
    update=pltpu.VMEM((CH, CW, R), F32),
    rows_send=pltpu.VMEM((2, 4, 8, R), jnp.int32),
    rows_in=pltpu.VMEM((2, 4, 8, R), jnp.int32),
    one_hot=pltpu.VMEM((2, 2, W, 4 * R), BF16),
    first_send=pltpu.VMEM((C, 2, 4, 2, CW, R), F32),
    first_in=pltpu.VMEM((C, 2, 4, 2, CW, R), F32),
    dense=pltpu.VMEM((C, 2, 2, CW, W), F32),
    second_in=pltpu.VMEM((C, 4, CW, W), F32),
    k_high=pltpu.VMEM((W, W), BF16),
    k_low=pltpu.VMEM((W, W), BF16),
    z_parent=pltpu.VMEM((W, W), F32),
    x_block=pltpu.VMEM((C, 2, 2, CW, W), F32),
    x_all=pltpu.VMEM((W, W), F32),
    pick_send=pltpu.VMEM((C, 2, 4, 2, CW, R), F32),
    pick_in_0=pltpu.VMEM((2, 4, 2, CW, R), F32),
    pick_in_1=pltpu.VMEM((2, 4, 2, CW, R), F32),
    pick_in_2=pltpu.VMEM((2, 4, 2, CW, R), F32),
    pick_in_3=pltpu.VMEM((2, 4, 2, CW, R), F32),
    v_send=pltpu.VMEM((C, CH, CW, R), F32),
    v_in=pltpu.VMEM((C, CH, CW, R), F32),
    panel_in=pltpu.VMEM((CH, R, W), F32),
    gain_high=pltpu.VMEM((CH, R, W), BF16),
    gain_low=pltpu.VMEM((CH, R, W), BF16),
    z_child=pltpu.VMEM((CH, W, W), F32),
    out_buf=pltpu.VMEM((CH, W, W), F32),
    load_sem=DMA((3, CH)),
    out_sem=DMA((2, CH)),
    y_s=DMA((C, CH)), y_r=DMA((C, CH)),
    p_s=DMA((CH,)), p_r=DMA((CH,)),
    i_s=DMA((2, 4)), i_r=DMA((2, 4)),
    s1_s=DMA((C, 2, 4)), s1_r=DMA((C, 2, 4)),
    s2_s=DMA((C, 3)), s2_r=DMA((C, 4)),
    t1_s=DMA((C, 4)), t1_r=DMA((C, 2, 2)),
    t2_s=DMA((C, 2, 4)), t2_r=DMA((C, 2, 4)),
    v_s=DMA((C, CH)), v_r=DMA((C, CH)),
)
NN = ((1,), (0,))
NT = ((1,), (1,))
TN = ((0,), (0,))


def split(value):
    high = value.astype(BF16)
    low = (value - high.astype(F32)).astype(BF16)
    return high, low


def dot(a, b, dims=NN):
    return lax.dot_general(a, b, (dims, ((), ())), preferred_element_type=F32)


def product(a, b, dims=NN):
    a_high, a_low = split(a)
    b_high, b_low = split(b)
    return dot(a_high, b_high, dims) + (dot(a_high, b_low, dims) + dot(a_low, b_high, dims))


def streamed(a, b_high, b_low, dims=NN):
    rows = a.shape[0]
    a_high, a_low = split(a)
    both = dot(jnp.concatenate([a_high, a_low], axis=0), b_high, dims)
    return both[:rows] + (both[rows:] + dot(a_high, b_low, dims))


def chosen(a, one_hot, dims=NN):
    rows = a.shape[0]
    a_high, a_low = split(a)
    both = dot(jnp.concatenate([a_high, a_low], axis=0), one_hot, dims)
    return both[:rows] + both[rows:]


def kernel(parent_ids, inverse_hbm, rhs_hbm, panels_hbm, rows_ref, pinv_ref, prhs_ref, child_out, parent_out, *scratch):
    ref = dict(zip(SCRATCH, scratch))
    inverse, rhs, panels, panel_high, panel_low = (ref[n] for n in ("inverse", "rhs", "panels", "panel_high", "panel_low"))
    y_send, y_in, update, rows_send, rows_in = (ref[n] for n in ("y_send", "y_in", "update", "rows_send", "rows_in"))
    one_hot, first_send, first_in, dense, second_in = (ref[n] for n in ("one_hot", "first_send", "first_in", "dense", "second_in"))
    k_high, k_low, z_parent, x_block, x_all = (ref[n] for n in ("k_high", "k_low", "z_parent", "x_block", "x_all"))
    pick_send, v_send, v_in, panel_in = (ref[n] for n in ("pick_send", "v_send", "v_in", "panel_in"))
    pick_in = [ref["pick_in_%d" % c] for c in range(C)]
    gain_high, gain_low, z_child, out_buf = (ref[n] for n in ("gain_high", "gain_low", "z_child", "out_buf"))
    load_sem, out_sem, y_s, y_r, p_s, p_r, i_s, i_r = (ref[n] for n in ("load_sem", "out_sem", "y_s", "y_r", "p_s", "p_r", "i_s", "i_r"))
    s1_s, s1_r, s2_s, s2_r, t1_s, t1_r = (ref[n] for n in ("s1_s", "s1_r", "s2_s", "s2_r", "t1_s", "t1_r"))
    t2_s, t2_r, v_s, v_r = (ref[n] for n in ("t2_s", "t2_r", "v_s", "v_r"))

    r = lax.axis_index("prow")
    q = lax.axis_index("pcol")
    z, core = r // 2, r % 2
    x, y = q // 4, q % 4
    cls = (x + y + core) % 2
    own_pos = jnp.where(cls == 0, y, x)
    other_pos = jnp.where(cls == 0, x, y)
    t_self = own_pos // 2
    first_pos = (x, y)

    def partner(j):
        m = j // 2
        step = jnp.where(m == 0, 2, jnp.where(m == 1, 1, jnp.where(m == 2, 3, 0)))
        return ((z + step) % 4) * 2 + (core + j + m // 3) % 2

    def each(first, last, action):
        def one(j, carry):
            action(j)
            return carry

        lax.fori_loop(first, last, one, 0)

    def first_dev(f, a):
        return (r, a * 4 + y) if f == 0 else (r, x * 4 + a)

    def own_dev(a):
        return (r, jnp.where(cls == 0, x * 4 + a, a * 4 + y))

    def other_dev(a):
        return (r, jnp.where(cls == 0, a * 4 + y, x * 4 + a))

    def remote(src, dst, send, recv, dev):
        return pltpu.make_async_remote_copy(
            src_ref=src, dst_ref=dst, send_sem=send, recv_sem=recv, device_id=dev, device_id_type=MESH
        )

    barrier = pltpu.get_barrier_semaphore()
    each(0, 7, lambda j: pl.semaphore_signal(barrier, inc=1, device_id=(partner(j), q), device_id_type=MESH))
    for f in range(2):
        for d in range(1, 4):
            pl.semaphore_signal(barrier, inc=1, device_id=first_dev(f, (first_pos[f] + d) % 4), device_id_type=MESH)

    def load(k):
        return (
            pltpu.make_async_copy(inverse_hbm.at[k], inverse.at[k], load_sem.at[0, k]),
            pltpu.make_async_copy(rhs_hbm.at[k], rhs.at[k], load_sem.at[1, k]),
        )

    def start_load(j):
        for copy in load(partner(j)):
            copy.start()

    each(0, 8, start_load)
    panel_load = pltpu.make_async_copy(panels_hbm, panels, load_sem.at[2, 0])
    panel_load.start()

    def y_copy(c, k):
        return remote(y_send.at[c, k], y_in.at[c, r], y_s.at[c, k], y_r.at[c, r], (k, q))

    def y_wait(c, s):
        return remote(y_send.at[c, s], y_in.at[c, s], y_s.at[c, s], y_r.at[c, s], (s, q))

    def forward(k):
        for copy in load(k):
            copy.wait()
        value = product(inverse[k], rhs[k]).T
        for c in range(C):
            y_send[c, k] = value[c * CW:(c + 1) * CW]

    def forward_step(j):
        forward(partner(j))
        y_copy(0, partner(j)).start()

    forward(partner(0))
    pl.semaphore_wait(barrier, 13)
    y_copy(0, partner(0)).start()
    each(1, 7, forward_step)
    forward(r)
    for c in range(C):
        y_in[c, r] = y_send[c, r]

    def y_follow(c):
        each(0, 7, lambda j: y_copy(c - 1, partner(j)).wait_send())
        each(0, 7, lambda j: y_copy(c, partner(j)).start())

    def parent_of(f, a, t):
        if f == 0:
            return a * 4 + (a + core) % 2 + 2 * t
        return ((a + core + 1) % 2 + 2 * t) * 4 + a

    def rows_copy(f, a):
        return remote(rows_send.at[f, a], rows_in.at[f, first_pos[f]], i_s.at[f, a], i_r.at[f, first_pos[f]], first_dev(f, a))

    def rows_wait(f, a):
        return remote(rows_send.at[f, a], rows_in.at[f, a], i_s.at[f, a], i_r.at[f, a], first_dev(f, a))

    def send_rows():
        for f in range(2):
            for a in range(4):
                for t in range(2):
                    p = parent_of(f, a, t)
                    listed = jnp.full((1, R), -1, jnp.int32)
                    for s in range(CH):
                        listed = jnp.where(parent_ids[s] == p, rows_ref[s:s + 1, :], listed)
                    rows_send[f, a, t:t + 1, :] = listed
                rows_send[f, a, 2:8, :] = jnp.zeros((6, R), jnp.int32)
            rows_in[f, first_pos[f]] = rows_send[f, first_pos[f]]
            for d in range(1, 4):
                rows_copy(f, (first_pos[f] + d) % 4).start()

    def split_panels():
        panel_load.wait()
        for s in range(CH):
            high, low = split(panels[s])
            panel_high[s] = high
            panel_low[s] = low

    def gram():
        value = product(pinv_ref[...], pinv_ref[...], TN)
        high, low = split(value)
        k_high[...] = high
        k_low[...] = low
        z_parent[...] = product(value, prhs_ref[...]).T

    def make_one_hot():
        places = lax.broadcasted_iota(jnp.int32, (W, R), 0)
        for f in range(2):
            for d in range(1, 4):
                rows_wait(f, (first_pos[f] + d) % 4).wait_recv()
            for a in range(4):
                for t in range(2):
                    matrix = jnp.where(places == rows_in[f, a, t:t + 1, :], 1.0, 0.0)
                    one_hot[f, t, :, a * R:(a + 1) * R] = matrix.astype(BF16)

    def first_copy(c, f, a):
        return remote(first_send.at[c, f, a], first_in.at[c, f, first_pos[f]], s1_s.at[c, f, a], s1_r.at[c, f, first_pos[f]], first_dev(f, a))

    def first_wait(c, f, a):
        return remote(first_send.at[c, f, a], first_in.at[c, f, a], s1_s.at[c, f, a], s1_r.at[c, f, a], first_dev(f, a))

    def step_update(c):
        def one(s):
            update[s] = streamed(y_in[c, s], panel_high[s], panel_low[s], NT)

        def arrived(j):
            s = partner(6 - j)
            y_wait(c, s).wait_recv()
            one(s)

        one(r)
        each(0, 7, arrived)
        for f in range(2):
            for a in range(4):
                for t in range(2):
                    p = parent_of(f, a, t)
                    slot = jnp.int32(0)
                    for s in range(1, CH):
                        slot = jnp.where(parent_ids[s] == p, s, slot)
                    first_send[c, f, a, t] = update[slot]
            first_in[c, f, first_pos[f]] = first_send[c, f, first_pos[f]]
            for d in (2, 1, 3):
                first_copy(c, f, (first_pos[f] + d) % 4).start()

    def second_own(c):
        a = (own_pos + 2) % 4
        return remote(dense.at[c, cls, 1 - t_self], second_in.at[c, own_pos], s2_s.at[c, 2], s2_r.at[c, own_pos], own_dev(a))

    def second_other(c, t):
        a = (other_pos + 1) % 2 + 2 * t
        return remote(dense.at[c, 1 - cls, t], second_in.at[c, other_pos], s2_s.at[c, t], s2_r.at[c, other_pos], other_dev(a))

    def second_wait(c, a):
        return remote(dense.at[c, 0, 0], second_in.at[c, a], s2_s.at[c, 0], s2_r.at[c, a], own_dev(a))

    def step_dense(c):
        for f in range(2):
            for d in (1, 3, 2):
                first_wait(c, f, (first_pos[f] + d) % 4).wait_recv()
            for t in range(2):
                blocks = jnp.concatenate([first_in[c, f, a, t] for a in range(4)], axis=1)
                dense[c, f, t] = chosen(blocks, one_hot[f, t], NT)
        second_own(c).start()
        for t in range(2):
            second_other(c, t).start()

    def x_copy(c, d):
        return remote(x_block.at[c, cls, t_self], x_block.at[c, cls, t_self], t1_s.at[c, d], t1_r.at[c, cls, t_self], own_dev((own_pos + d) % 4))

    def x_wait_own(c):
        return remote(x_block.at[c, cls, 1 - t_self], x_block.at[c, cls, 1 - t_self], t1_s.at[c, 1], t1_r.at[c, cls, 1 - t_self], own_dev((own_pos + 2) % 4))

    def x_wait_other(c, t):
        a = (other_pos + 1) % 2 + 2 * t
        return remote(x_block.at[c, 1 - cls, t], x_block.at[c, 1 - cls, t], t1_s.at[c, 1], t1_r.at[c, 1 - cls, t], other_dev(a))

    def step_parent(c):
        total = dense[c, cls, t_self]
        for d in (1, 3, 2):
            a = (own_pos + d) % 4
            second_wait(c, a).wait_recv()
            total = total + second_in[c, a]
        value = z_parent[c * CW:(c + 1) * CW] - streamed(total, k_high[...], k_low[...])
        x_block[c, cls, t_self] = value
        for d in (2, 1, 3):
            x_copy(c, d).start()
        x_all[c * CW:(c + 1) * CW] = value

    def pick_copy(c, f, a):
        return remote(pick_send.at[c, f, a], pick_in[c].at[f, first_pos[f]], t2_s.at[c, f, a], t2_r.at[c, f, first_pos[f]], first_dev(f, a))

    def pick_wait(c, f, a):
        return remote(pick_send.at[c, f, a], pick_in[c].at[f, a], t2_s.at[c, f, a], t2_r.at[c, f, a], first_dev(f, a))

    def step_pick(c):
        for t in range(2):
            x_wait_other(c, t).wait_recv()
        x_wait_own(c).wait_recv()
        for f in range(2):
            for t in range(2):
                picked = chosen(x_block[c, f, t], one_hot[f, t])
                for a in range(4):
                    pick_send[c, f, a, t] = picked[:, a * R:(a + 1) * R]
            pick_in[c][f, first_pos[f]] = pick_send[c, f, first_pos[f]]
            for d in (2, 1, 3):
                pick_copy(c, f, (first_pos[f] + d) % 4).start()

    def v_copy(c, s):
        return remote(v_send.at[c, s], v_in.at[c, r], v_s.at[c, s], v_r.at[c, r], (s, q))

    def v_wait(c, s):
        return remote(v_send.at[c, s], v_in.at[c, s], v_s.at[c, s], v_r.at[c, s], (s, q))

    def step_return(c):
        for f in range(2):
            for d in (1, 3, 2):
                pick_wait(c, f, (first_pos[f] + d) % 4).wait_recv()

        def one(s):
            p = parent_ids[s]
            x_p, y_p = p // 4, p % 4
            f = (x_p + y_p + core) % 2
            a = jnp.where(f == 0, x_p, y_p)
            t = jnp.where(f == 0, y_p, x_p) // 2
            v_send[c, s] = pick_in[c][f, a, t]

        def go(j):
            s = partner(j)
            one(s)
            v_copy(c, s).start()

        each(0, 7, go)
        one(r)
        v_in[c, r] = v_send[c, r]

    def panel_copy(k):
        return remote(panels.at[k], panel_in.at[r], p_s.at[k], p_r.at[r], (k, q))

    def panel_wait(s):
        return remote(panels.at[s], panel_in.at[s], p_s.at[s], p_r.at[s], (s, q))

    def send_panels():
        each(0, 7, lambda j: y_copy(C - 1, partner(j)).wait_send())
        each(0, 7, lambda j: panel_copy(partner(j)).start())
        panel_in[r] = panels[r]

    def gains():
        each(0, 7, lambda j: panel_wait(partner(6 - j)).wait_recv())

        def one(s):
            high, low = split(product(panel_in[s], inverse[s]))
            gain_high[s] = high
            gain_low[s] = low

        each(0, CH, one)

    def solved():
        def one(k):
            value = jnp.concatenate([y_send[c, k] for c in range(C)], axis=0)
            z_child[k] = product(value, inverse[k])

        each(0, CH, one)

    def out_copy(h, k):
        return pltpu.make_async_copy(out_buf.at[k, :, pl.ds(h * R, R)], child_out.at[k, :, pl.ds(h * R, R)], out_sem.at[h, k])

    def step_final(c):
        def one(s):
            part = pl.ds(c * CW, CW)
            value = z_child[s, part] - streamed(v_in[c, s], gain_high[s], gain_low[s])
            if c % 2 == 0:
                z_child[s, part] = value
            else:
                both = jnp.concatenate([z_child[s, pl.ds((c - 1) * CW, CW)], value], axis=0)
                out_buf[s, :, c // 2 * R:(c // 2 + 1) * R] = both.T
                out_copy(c // 2, s).start()

        def arrived(j):
            s = partner(6 - j)
            v_wait(c, s).wait_recv()
            one(s)

        one(r)
        each(0, 7, arrived)

    send_rows()
    split_panels()
    gram()
    make_one_hot()

    y_follow(1)
    step_update(0)
    solved()
    step_dense(0)
    y_follow(2)
    step_update(1)
    step_parent(0)
    step_dense(1)
    y_follow(3)
    step_update(2)
    step_pick(0)
    step_parent(1)
    step_dense(2)
    send_panels()
    step_update(3)
    step_return(0)
    step_pick(1)
    step_parent(2)
    step_dense(3)
    step_return(1)
    step_pick(2)
    step_parent(3)
    parent_out[...] = x_all[...].T
    step_return(2)
    step_pick(3)
    gains()
    step_final(0)
    step_final(1)
    step_return(3)
    step_final(2)
    step_final(3)

    def z_done(j):
        k = partner(j)
        panel_copy(k).wait_send()
        for c in range(C):
            v_copy(c, k).wait_send()

    each(0, 7, z_done)
    for f in range(2):
        for d in range(1, 4):
            a = (first_pos[f] + d) % 4
            rows_copy(f, a).wait_send()
            for c in range(C):
                first_copy(c, f, a).wait_send()
                pick_copy(c, f, a).wait_send()
    for c in range(C):
        second_own(c).wait_send()
        for t in range(2):
            second_other(c, t).wait_send()
        for d in range(1, 4):
            x_copy(c, d).wait_send()

    def out_done(k):
        for h in range(2):
            out_copy(h, k).wait()

    each(0, CH, out_done)


def body(child_inverse, child_rhs, panels, panel_parent, panel_rows, parent_inverse, parent_rhs):
    vmem = pl.BlockSpec(memory_space=pltpu.VMEM)
    anywhere = pl.BlockSpec(memory_space=pl.ANY)
    child, parent = pl.pallas_call(
        kernel,
        out_shape=(jax.ShapeDtypeStruct((CH, W, W), F32), jax.ShapeDtypeStruct((W, W), F32)),
        in_specs=[pl.BlockSpec(memory_space=pltpu.SMEM), anywhere, anywhere, anywhere, vmem, vmem, vmem],
        out_specs=(anywhere, vmem),
        scratch_shapes=list(SCRATCH.values()),
        compiler_params=pltpu.CompilerParams(collective_id=0, has_side_effects=True, vmem_limit_bytes=56 << 20),
        cost_estimate=pl.CostEstimate(flops=2 * 2100 * 10**6, bytes_accessed=8 << 20, transcendentals=0),
    )(
        panel_parent.reshape(CH), child_inverse[0, 0], child_rhs[0, 0], panels[0, 0], panel_rows[0, 0],
        parent_inverse[0, 0], parent_rhs[0, 0],
    )
    return child[None, None], parent[None, None]


def solution(mesh):
    placed = (
        P("prow", "pcol", None, None, None),
        P("prow", "pcol", None, None, None),
        P("prow", "pcol", None, None, None),
        P("prow", "pcol", None, None),
        P("prow", "pcol", None, None),
        P("prow", "pcol", None, None),
        P("prow", "pcol", None, None),
    )
    return jax.shard_map(
        body,
        mesh=mesh,
        in_specs=placed,
        out_specs=(P("prow", "pcol", None, None, None), P("prow", "pcol", None, None)),
        check_vma=False,
    )
```

time: 89.2 us -> 81.3 us (0.911)
  Pallas kernels: 84.6 us -> 76.7 us
    pallas_call x1, Pallas kernels: 84.6 us -> 76.7 us  [body(): pl.pallas_call(kernel, out_shape=(jax.ShapeDtypeStruct((CH, W, W), F32),...]
where the time goes in v2:
time: 81.3 us; the launch traced here: 81.2 us
  Pallas kernels  76.7 us (94%)
  local copies, waits for them, and re-layouts  3.79 us (5%)
    pallas_call x1, Pallas kernels, body(): pl.pallas_call(kernel, out_shape=(jax.ShapeDtypeStruct((CH, W, W), F32),...  76.7 us
    unnamed x4, local copies, waits for them, and re-layouts  3.79 us

profile of v2, /device:TPU:1, one launch (start us, length us, event | category | flops | bytes accessed | tf_op | source)
XLA Modules:
  0.0 81.2 jit_solution(15737126036452386269)
XLA Ops:
  0.6 76.7 %shard_map.86 = (f32[8,256,256]{2,1,0:T(8,128)}, f32[256,256]{1,0:T(8,128)}) custom-call(s32[8]{0:T(128)} %bitcast.17, f32[8,256,256]{2,1,0:T(8,128)} %bitcast.11, f32[8,256,256]{2,1,0:T(8,128)} %bitcast.12, f32[8,128,256]{2,1,0:T(8,128)} %bitcast.13, s32[8,128]{1,0:T(8,128)} %bitcast.16, f32[256,256]{1,0:T(8,128)} %bitcast.14, f32[256,256]{1,0:T(8,128)} %bitcast.15), custom_call_target="tpu_custom_call" | custom-call | flops 4200000000 | bytes 8388608 | tf_op jit(solution)/shard_map/pallas_call | solution.py:482
  77.4 0.0 copy-start
  77.4 3.1 %copy.11 = f32[1,1,8,256,256]{4,3,2,1,0:T(8,128)} copy(f32[1,1,8,256,256]{4,3,2,1,0:T(8,128)} %bitcast.9) | data formatting | bytes 4194304
  80.5 0.0 copy-done
  80.5 0.7 copy.12
Async XLA Ops:
  77.4 3.1 %copy-start = (f32[256,256]{1,0:T(8,128)S(1)}, f32[256,256]{1,0:T(8,128)}, u32[]{:S(2)}) copy-start(f32[256,256]{1,0:T(8,128)} %get-tuple-element.5) | copy-start | bytes 786436

commit v3 on v2

v3 whole, which is shorter than its diff:
```python
import jax
import jax.numpy as jnp
from jax import lax
from jax.experimental import pallas as pl
from jax.experimental.pallas import tpu as pltpu
from jax.sharding import PartitionSpec as P

MESH = pl.DeviceIdType.MESH
F32 = jnp.float32
BF16 = jnp.bfloat16
DMA = pltpu.SemaphoreType.DMA
W = 256
R = 128
CH = 8
WIDTHS = [64, 64, 64, 64]
C = len(WIDTHS)
STARTS = [sum(WIDTHS[:c]) for c in range(C)]

SCRATCH = dict(
    inverse=pltpu.VMEM((CH, W, W), F32),
    rhs=pltpu.VMEM((CH, W, W), F32),
    panels=pltpu.VMEM((CH, R, W), F32),
    rows=pltpu.VMEM((CH, R), jnp.int32),
    pinv=pltpu.VMEM((W, W), F32),
    prhs=pltpu.VMEM((W, W), F32),
    panel_high=pltpu.VMEM((CH, R, W), BF16),
    panel_low=pltpu.VMEM((CH, R, W), BF16),
    rows_send=pltpu.VMEM((2, 4, 8, R), jnp.int32),
    rows_in=pltpu.VMEM((2, 4, 8, R), jnp.int32),
    one_hot=pltpu.VMEM((2, 2, W, 4 * R), BF16),
    k_high=pltpu.VMEM((W, W), BF16),
    k_low=pltpu.VMEM((W, W), BF16),
    z_parent=pltpu.VMEM((W, W), F32),
    x_all=pltpu.VMEM((W, W), F32),
    panel_in=pltpu.VMEM((CH, R, W), F32),
    gain_high=pltpu.VMEM((CH, R, W), BF16),
    gain_low=pltpu.VMEM((CH, R, W), BF16),
    z_child=pltpu.VMEM((CH, W, W), F32),
    out_buf=pltpu.VMEM((CH, W, W), F32),
    load_sem=DMA((3, CH)),
    out_sem=DMA((3, CH)),
    y_s=DMA((C, CH)), y_r=DMA((C, CH)),
    p_s=DMA((CH,)), p_r=DMA((CH,)),
    i_s=DMA((2, 4)), i_r=DMA((2, 4)),
    s1_s=DMA((C, 2, 4)), s1_r=DMA((C, 2, 4)),
    s2_s=DMA((C, 3)), s2_r=DMA((C, 4)),
    t1_s=DMA((C, 4)), t1_r=DMA((C, 2, 2)),
    t2_s=DMA((C, 2, 4)), t2_r=DMA((C, 2, 4)),
    v_s=DMA((C, CH)), v_r=DMA((C, CH)),
)
CHUNKED = dict(
    y_send=(CH, None, W),
    y_in=(CH, None, W),
    update=(CH, None, R),
    first_send=(2, 4, 2, None, R),
    first_in=(2, 4, 2, None, R),
    dense=(2, 2, None, W),
    second_in=(4, None, W),
    x_block=(2, 2, None, W),
    pick_send=(2, 4, 2, None, R),
    pick_in=(2, 4, 2, None, R),
    v_send=(CH, None, R),
    v_in=(CH, None, R),
)
for name, shape in CHUNKED.items():
    for c in range(C):
        SCRATCH[name + str(c)] = pltpu.VMEM(tuple(WIDTHS[c] if n is None else n for n in shape), F32)
NN = ((1,), (0,))
NT = ((1,), (1,))
TN = ((0,), (0,))

ORDER = [
    "solved", "U0", "U1", "D0", "U2", "D1", "P0", "U3", "D2", "P1",
    "K0", "D3", "P2", "K1", "gains", "R0", "P3", "parent", "K2", "F0",
    "R1", "K3", "R2", "F1", "R3", "F2", "F3",
]


def split(value):
    high = value.astype(BF16)
    low = (value - high.astype(F32)).astype(BF16)
    return high, low


def dot(a, b, dims=NN):
    return lax.dot_general(a, b, (dims, ((), ())), preferred_element_type=F32)


def product(a, b, dims=NN):
    a_high, a_low = split(a)
    b_high, b_low = split(b)
    return dot(a_high, b_high, dims) + (dot(a_high, b_low, dims) + dot(a_low, b_high, dims))


def streamed(a, b_high, b_low, dims=NN):
    rows = a.shape[0]
    a_high, a_low = split(a)
    both = dot(jnp.concatenate([a_high, a_low], axis=0), b_high, dims)
    return both[:rows] + (both[rows:] + dot(a_high, b_low, dims))


def chosen(a, one_hot, dims=NN):
    rows = a.shape[0]
    a_high, a_low = split(a)
    both = dot(jnp.concatenate([a_high, a_low], axis=0), one_hot, dims)
    return both[:rows] + both[rows:]


def kernel(parent_ids, inverse_hbm, rhs_hbm, panels_hbm, rows_hbm, pinv_hbm, prhs_hbm, child_out, parent_out, *scratch):
    ref = dict(zip(SCRATCH, scratch))
    inverse = ref["inverse"]
    rhs = ref["rhs"]
    panels = ref["panels"]
    rows = ref["rows"]
    pinv = ref["pinv"]
    prhs = ref["prhs"]
    panel_high = ref["panel_high"]
    panel_low = ref["panel_low"]
    rows_send = ref["rows_send"]
    rows_in = ref["rows_in"]
    one_hot = ref["one_hot"]
    k_high = ref["k_high"]
    k_low = ref["k_low"]
    z_parent = ref["z_parent"]
    x_all = ref["x_all"]
    panel_in = ref["panel_in"]
    gain_high = ref["gain_high"]
    gain_low = ref["gain_low"]
    z_child = ref["z_child"]
    out_buf = ref["out_buf"]
    load_sem = ref["load_sem"]
    out_sem = ref["out_sem"]
    y_s = ref["y_s"]
    y_r = ref["y_r"]
    p_s = ref["p_s"]
    p_r = ref["p_r"]
    i_s = ref["i_s"]
    i_r = ref["i_r"]
    s1_s = ref["s1_s"]
    s1_r = ref["s1_r"]
    s2_s = ref["s2_s"]
    s2_r = ref["s2_r"]
    t1_s = ref["t1_s"]
    t1_r = ref["t1_r"]
    t2_s = ref["t2_s"]
    t2_r = ref["t2_r"]
    v_s = ref["v_s"]
    v_r = ref["v_r"]
    y_send = [ref["y_send" + str(c)] for c in range(C)]
    y_in = [ref["y_in" + str(c)] for c in range(C)]
    update = [ref["update" + str(c)] for c in range(C)]
    first_send = [ref["first_send" + str(c)] for c in range(C)]
    first_in = [ref["first_in" + str(c)] for c in range(C)]
    dense = [ref["dense" + str(c)] for c in range(C)]
    second_in = [ref["second_in" + str(c)] for c in range(C)]
    x_block = [ref["x_block" + str(c)] for c in range(C)]
    pick_send = [ref["pick_send" + str(c)] for c in range(C)]
    pick_in = [ref["pick_in" + str(c)] for c in range(C)]
    v_send = [ref["v_send" + str(c)] for c in range(C)]
    v_in = [ref["v_in" + str(c)] for c in range(C)]

    r = lax.axis_index("prow")
    q = lax.axis_index("pcol")
    z, core = r // 2, r % 2
    x, y = q // 4, q % 4
    cls = (x + y + core) % 2
    own_pos = jnp.where(cls == 0, y, x)
    other_pos = jnp.where(cls == 0, x, y)
    t_self = own_pos // 2
    first_pos = (x, y)

    def partner(j):
        m = j // 2
        step = jnp.where(m == 0, 2, jnp.where(m == 1, 1, jnp.where(m == 2, 3, 0)))
        return ((z + step) % 4) * 2 + (core + j + m // 3) % 2

    def each(first, last, action, unroll=1):
        def one(j, carry):
            action(j)
            return carry

        lax.fori_loop(first, last, one, 0, unroll=unroll)

    def first_dev(f, a):
        return (r, a * 4 + y) if f == 0 else (r, x * 4 + a)

    def own_dev(a):
        return (r, jnp.where(cls == 0, x * 4 + a, a * 4 + y))

    def other_dev(a):
        return (r, jnp.where(cls == 0, a * 4 + y, x * 4 + a))

    def remote(src, dst, send, recv, dev):
        return pltpu.make_async_remote_copy(
            src_ref=src, dst_ref=dst, send_sem=send, recv_sem=recv, device_id=dev, device_id_type=MESH
        )

    barrier = pltpu.get_barrier_semaphore()
    each(0, 7, lambda j: pl.semaphore_signal(barrier, inc=1, device_id=(partner(j), q), device_id_type=MESH))
    for f in range(2):
        for d in range(1, 4):
            pl.semaphore_signal(barrier, inc=1, device_id=first_dev(f, (first_pos[f] + d) % 4), device_id_type=MESH)

    def load(k):
        return (
            pltpu.make_async_copy(inverse_hbm.at[k], inverse.at[k], load_sem.at[0, k]),
            pltpu.make_async_copy(rhs_hbm.at[k], rhs.at[k], load_sem.at[1, k]),
        )

    def start_load(j):
        for copy in load(partner(j)):
            copy.start()

    each(0, 8, start_load)
    panel_load = pltpu.make_async_copy(panels_hbm, panels, load_sem.at[2, 0])
    rows_load = pltpu.make_async_copy(rows_hbm, rows, load_sem.at[2, 1])
    pinv_load = pltpu.make_async_copy(pinv_hbm, pinv, load_sem.at[2, 2])
    prhs_load = pltpu.make_async_copy(prhs_hbm, prhs, load_sem.at[2, 3])
    for copy in (rows_load, panel_load, pinv_load, prhs_load):
        copy.start()

    def y_copy(c, k):
        return remote(y_send[c].at[k], y_in[c].at[r], y_s.at[c, k], y_r.at[c, r], (k, q))

    def y_wait(c, s):
        return remote(y_send[c].at[s], y_in[c].at[s], y_s.at[c, s], y_r.at[c, s], (s, q))

    def forward(k):
        for copy in load(k):
            copy.wait()
        value = product(inverse[k], rhs[k]).T
        for c in range(C):
            y_send[c][k] = value[STARTS[c]:STARTS[c] + WIDTHS[c]]

    def forward_step(j):
        forward(partner(j))
        y_copy(0, partner(j)).start()

    forward(partner(0))
    pl.semaphore_wait(barrier, 13)
    y_copy(0, partner(0)).start()
    each(1, 7, forward_step)
    forward(r)
    for c in range(C):
        y_in[c][r] = y_send[c][r]

    def y_follow(c):
        each(0, 7, lambda j: y_copy(c, partner(j)).start())

    def parent_of(f, a, t):
        if f == 0:
            return a * 4 + (a + core) % 2 + 2 * t
        return ((a + core + 1) % 2 + 2 * t) * 4 + a

    def rows_copy(f, a):
        return remote(rows_send.at[f, a], rows_in.at[f, first_pos[f]], i_s.at[f, a], i_r.at[f, first_pos[f]], first_dev(f, a))

    def rows_wait(f, a):
        return remote(rows_send.at[f, a], rows_in.at[f, a], i_s.at[f, a], i_r.at[f, a], first_dev(f, a))

    def send_rows():
        rows_load.wait()
        for f in range(2):
            for a in range(4):
                for t in range(2):
                    p = parent_of(f, a, t)
                    listed = jnp.full((1, R), -1, jnp.int32)
                    for s in range(CH):
                        listed = jnp.where(parent_ids[s] == p, rows[s:s + 1, :], listed)
                    rows_send[f, a, t:t + 1, :] = listed
                rows_send[f, a, 2:8, :] = jnp.zeros((6, R), jnp.int32)
            rows_in[f, first_pos[f]] = rows_send[f, first_pos[f]]
            for d in range(1, 4):
                rows_copy(f, (first_pos[f] + d) % 4).start()

    def split_panels():
        panel_load.wait()
        for s in range(CH):
            high, low = split(panels[s])
            panel_high[s] = high
            panel_low[s] = low

    def gram():
        pinv_load.wait()
        prhs_load.wait()
        value = product(pinv[...], pinv[...], TN)
        high, low = split(value)
        k_high[...] = high
        k_low[...] = low
        z_parent[...] = product(value, prhs[...]).T

    def make_one_hot():
        places = lax.broadcasted_iota(jnp.int32, (W, R), 0)
        for f in range(2):
            for d in range(1, 4):
                rows_wait(f, (first_pos[f] + d) % 4).wait_recv()
            for a in range(4):
                for t in range(2):
                    matrix = jnp.where(places == rows_in[f, a, t:t + 1, :], 1.0, 0.0)
                    one_hot[f, t, :, a * R:(a + 1) * R] = matrix.astype(BF16)

    def first_copy(c, f, a):
        return remote(first_send[c].at[f, a], first_in[c].at[f, first_pos[f]], s1_s.at[c, f, a], s1_r.at[c, f, first_pos[f]], first_dev(f, a))

    def first_wait(c, f, a):
        return remote(first_send[c].at[f, a], first_in[c].at[f, a], s1_s.at[c, f, a], s1_r.at[c, f, a], first_dev(f, a))

    def step_update(c):
        def one(s):
            update[c][s] = streamed(y_in[c][s], panel_high[s], panel_low[s], NT)

        each(0, 5, lambda j: y_wait(c, partner(6 - j)).wait_recv())
        each(0, 6, lambda j: one(partner(7 - j)), 6)
        each(0, 2, lambda j: y_wait(c, partner(j)).wait_recv())
        each(0, 2, lambda j: one(partner(j)), 2)
        for f in range(2):
            for a in range(4):
                for t in range(2):
                    p = parent_of(f, a, t)
                    slot = jnp.int32(0)
                    for s in range(1, CH):
                        slot = jnp.where(parent_ids[s] == p, s, slot)
                    first_send[c][f, a, t] = update[c][slot]
            first_in[c][f, first_pos[f]] = first_send[c][f, first_pos[f]]
            for d in (2, 1, 3):
                first_copy(c, f, (first_pos[f] + d) % 4).start()

    def second_own(c):
        a = (own_pos + 2) % 4
        return remote(dense[c].at[cls, 1 - t_self], second_in[c].at[own_pos], s2_s.at[c, 2], s2_r.at[c, own_pos], own_dev(a))

    def second_other(c, t):
        a = (other_pos + 1) % 2 + 2 * t
        return remote(dense[c].at[1 - cls, t], second_in[c].at[other_pos], s2_s.at[c, t], s2_r.at[c, other_pos], other_dev(a))

    def second_wait(c, a):
        return remote(dense[c].at[0, 0], second_in[c].at[a], s2_s.at[c, 0], s2_r.at[c, a], own_dev(a))

    def step_dense(c):
        for f in range(2):
            for d in (1, 3, 2):
                first_wait(c, f, (first_pos[f] + d) % 4).wait_recv()
            for t in range(2):
                blocks = jnp.concatenate([first_in[c][f, a, t] for a in range(4)], axis=1)
                dense[c][f, t] = chosen(blocks, one_hot[f, t], NT)
        second_own(c).start()
        for t in range(2):
            second_other(c, t).start()

    def x_copy(c, d):
        return remote(x_block[c].at[cls, t_self], x_block[c].at[cls, t_self], t1_s.at[c, d], t1_r.at[c, cls, t_self], own_dev((own_pos + d) % 4))

    def x_wait_own(c):
        return remote(x_block[c].at[cls, 1 - t_self], x_block[c].at[cls, 1 - t_self], t1_s.at[c, 1], t1_r.at[c, cls, 1 - t_self], own_dev((own_pos + 2) % 4))

    def x_wait_other(c, t):
        a = (other_pos + 1) % 2 + 2 * t
        return remote(x_block[c].at[1 - cls, t], x_block[c].at[1 - cls, t], t1_s.at[c, 1], t1_r.at[c, 1 - cls, t], other_dev(a))

    def step_parent(c):
        total = dense[c][cls, t_self]
        for d in (1, 3, 2):
            a = (own_pos + d) % 4
            second_wait(c, a).wait_recv()
            total = total + second_in[c][a]
        value = z_parent[STARTS[c]:STARTS[c] + WIDTHS[c]] - streamed(total, k_high[...], k_low[...])
        x_block[c][cls, t_self] = value
        for d in (2, 1, 3):
            x_copy(c, d).start()
        x_all[STARTS[c]:STARTS[c] + WIDTHS[c]] = value

    def pick_copy(c, f, a):
        return remote(pick_send[c].at[f, a], pick_in[c].at[f, first_pos[f]], t2_s.at[c, f, a], t2_r.at[c, f, first_pos[f]], first_dev(f, a))

    def pick_wait(c, f, a):
        return remote(pick_send[c].at[f, a], pick_in[c].at[f, a], t2_s.at[c, f, a], t2_r.at[c, f, a], first_dev(f, a))

    def step_pick(c):
        for t in range(2):
            x_wait_other(c, t).wait_recv()
        x_wait_own(c).wait_recv()
        for f in range(2):
            for t in range(2):
                picked = chosen(x_block[c][f, t], one_hot[f, t])
                for a in range(4):
                    pick_send[c][f, a, t] = picked[:, a * R:(a + 1) * R]
            pick_in[c][f, first_pos[f]] = pick_send[c][f, first_pos[f]]
            for d in (2, 1, 3):
                pick_copy(c, f, (first_pos[f] + d) % 4).start()

    def v_copy(c, s):
        return remote(v_send[c].at[s], v_in[c].at[r], v_s.at[c, s], v_r.at[c, r], (s, q))

    def v_wait(c, s):
        return remote(v_send[c].at[s], v_in[c].at[s], v_s.at[c, s], v_r.at[c, s], (s, q))

    def step_return(c):
        for f in range(2):
            for d in (1, 3, 2):
                pick_wait(c, f, (first_pos[f] + d) % 4).wait_recv()

        def one(s):
            p = parent_ids[s]
            x_p, y_p = p // 4, p % 4
            f = (x_p + y_p + core) % 2
            a = jnp.where(f == 0, x_p, y_p)
            t = jnp.where(f == 0, y_p, x_p) // 2
            v_send[c][s] = pick_in[c][f, a, t]

        def go(j):
            s = partner(j)
            one(s)
            v_copy(c, s).start()

        each(0, 7, go)
        one(r)
        v_in[c][r] = v_send[c][r]

    def panel_copy(k):
        return remote(panels.at[k], panel_in.at[r], p_s.at[k], p_r.at[r], (k, q))

    def panel_wait(s):
        return remote(panels.at[s], panel_in.at[s], p_s.at[s], p_r.at[s], (s, q))

    def send_panels():
        each(0, 7, lambda j: panel_copy(partner(j)).start())
        panel_in[r] = panels[r]

    def gains():
        each(0, 7, lambda j: panel_wait(partner(6 - j)).wait_recv())

        def one(s):
            high, low = split(product(panel_in[s], inverse[s]))
            gain_high[s] = high
            gain_low[s] = low

        each(0, CH, one, 4)

    def solved():
        def one(k):
            value = jnp.concatenate([y_send[c][k] for c in range(C)], axis=0)
            z_child[k] = product(value, inverse[k])

        each(0, CH, one, 4)

    def out_copy(h, k):
        return pltpu.make_async_copy(out_buf.at[k, :, pl.ds(h * R, R)], child_out.at[k, :, pl.ds(h * R, R)], out_sem.at[h, k])

    def step_final(c):
        start = STARTS[c]
        end = start + WIDTHS[c]
        half = start // R

        def one(s):
            value = z_child[s, start:end] - streamed(v_in[c][s], gain_high[s], gain_low[s])
            if end % R:
                z_child[s, start:end] = value
            else:
                if start % R:
                    value = jnp.concatenate([z_child[s, half * R:start], value], axis=0)
                out_buf[s, :, half * R:(half + 1) * R] = value.T
                out_copy(half, s).start()

        each(0, 5, lambda j: v_wait(c, partner(6 - j)).wait_recv())
        each(0, 6, lambda j: one(partner(7 - j)), 6)
        each(0, 2, lambda j: v_wait(c, partner(j)).wait_recv())
        each(0, 2, lambda j: one(partner(j)), 2)

    x_out = pltpu.make_async_copy(x_all, parent_out, out_sem.at[2, 0])

    def parent_result():
        x_all[...] = x_all[...].T
        x_out.start()

    steps = dict(U=step_update, D=step_dense, P=step_parent, K=step_pick, R=step_return, F=step_final)
    send_rows()
    for c in range(1, C):
        y_follow(c)
    split_panels()
    send_panels()
    gram()
    make_one_hot()
    for step in ORDER:
        if step == "solved":
            solved()
        elif step == "gains":
            gains()
        elif step == "parent":
            parent_result()
        else:
            steps[step[0]](int(step[1:]))

    def z_done(j):
        k = partner(j)
        panel_copy(k).wait_send()
        for c in range(C):
            y_copy(c, k).wait_send()
        for c in range(C):
            v_copy(c, k).wait_send()

    each(0, 7, z_done)
    for f in range(2):
        for d in range(1, 4):
            a = (first_pos[f] + d) % 4
            rows_copy(f, a).wait_send()
            for c in range(C):
                first_copy(c, f, a).wait_send()
                pick_copy(c, f, a).wait_send()
    for c in range(C):
        second_own(c).wait_send()
        for t in range(2):
            second_other(c, t).wait_send()
        for d in range(1, 4):
            x_copy(c, d).wait_send()

    def out_done(k):
        for h in range(2):
            out_copy(h, k).wait()

    each(0, CH, out_done)
    x_out.wait()


def body(child_inverse, child_rhs, panels, panel_parent, panel_rows, parent_inverse, parent_rhs):
    anywhere = pl.BlockSpec(memory_space=pl.ANY)
    child, parent = pl.pallas_call(
        kernel,
        out_shape=(jax.ShapeDtypeStruct((CH, W, W), F32), jax.ShapeDtypeStruct((W, W), F32)),
        in_specs=[pl.BlockSpec(memory_space=pltpu.SMEM)] + [anywhere] * 6,
        out_specs=(anywhere, anywhere),
        scratch_shapes=list(SCRATCH.values()),
        compiler_params=pltpu.CompilerParams(collective_id=0, has_side_effects=True, vmem_limit_bytes=56 << 20),
        cost_estimate=pl.CostEstimate(flops=2 * 2100 * 10**6, bytes_accessed=8 << 20, transcendentals=0),
    )(
        panel_parent.reshape(CH), child_inverse[0, 0], child_rhs[0, 0], panels[0, 0], panel_rows[0, 0],
        parent_inverse[0, 0], parent_rhs[0, 0],
    )
    return child[None, None], parent[None, None]


def solution(mesh):
    placed = (
        P("prow", "pcol", None, None, None),
        P("prow", "pcol", None, None, None),
        P("prow", "pcol", None, None, None),
        P("prow", "pcol", None, None),
        P("prow", "pcol", None, None),
        P("prow", "pcol", None, None),
        P("prow", "pcol", None, None),
    )
    return jax.shard_map(
        body,
        mesh=mesh,
        in_specs=placed,
        out_specs=(P("prow", "pcol", None, None, None), P("prow", "pcol", None, None)),
        check_vma=False,
    )
```

time: 81.3 us -> 74.1 us (0.911)
  Pallas kernels: 76.7 us -> 69.5 us
    pallas_call x1, Pallas kernels: 76.7 us -> 69.5 us  [body(): pl.pallas_call(kernel, out_shape=(jax.ShapeDtypeStruct((CH, W, W), F32),...]
where the time goes in v3:
time: 74.1 us; the launch traced here: 74 us
  Pallas kernels  69.5 us (94%)
  local copies, waits for them, and re-layouts  3.79 us (5%)
    pallas_call x1, Pallas kernels, body(): pl.pallas_call(kernel, out_shape=(jax.ShapeDtypeStruct((CH, W, W), F32),...  69.5 us
    unnamed x4, local copies, waits for them, and re-layouts  3.79 us

profile of v3, /device:TPU:1, one launch (start us, length us, event | category | flops | bytes accessed | tf_op | source)
XLA Modules:
  0.0 74.0 jit_solution(1095951780096884483)
XLA Ops:
  0.6 69.5 %shard_map.86 = (f32[8,256,256]{2,1,0:T(8,128)}, f32[256,256]{1,0:T(8,128)}) custom-call(s32[8]{0:T(128)} %bitcast.17, f32[8,256,256]{2,1,0:T(8,128)} %bitcast.11, f32[8,256,256]{2,1,0:T(8,128)} %bitcast.12, f32[8,128,256]{2,1,0:T(8,128)} %bitcast.13, s32[8,128]{1,0:T(8,128)} %bitcast.16, f32[256,256]{1,0:T(8,128)} %bitcast.14, f32[256,256]{1,0:T(8,128)} %bitcast.15), custom_call_target="tpu_custom_call" | custom-call | flops 4200000000 | bytes 8388608 | tf_op jit(solution)/shard_map/pallas_call | solution.py:526
  70.2 0.0 copy-start
  70.2 3.1 %copy.11 = f32[1,1,8,256,256]{4,3,2,1,0:T(8,128)} copy(f32[1,1,8,256,256]{4,3,2,1,0:T(8,128)} %bitcast.9) | data formatting | bytes 4194304
  73.3 0.0 copy-done
  73.3 0.7 copy.12
Async XLA Ops:
  70.2 3.1 %copy-start = (f32[256,256]{1,0:T(8,128)S(1)}, f32[256,256]{1,0:T(8,128)}, u32[]{:S(2)}) copy-start(f32[256,256]{1,0:T(8,128)} %get-tuple-element.5) | copy-start | bytes 786436

commit v4 on v3

--- a/solution.py
+++ b/solution.py
@@ -12,7 +12,7 @@
 W = 256
 R = 128
 CH = 8
-WIDTHS = [64, 64, 64, 64]
+WIDTHS = [32, 32, 64, 64, 32, 32]
 C = len(WIDTHS)
 STARTS = [sum(WIDTHS[:c]) for c in range(C)]
 
@@ -39,14 +39,14 @@
     out_buf=pltpu.VMEM((CH, W, W), F32),
     load_sem=DMA((3, CH)),
     out_sem=DMA((3, CH)),
-    y_s=DMA((C, CH)), y_r=DMA((C, CH)),
-    p_s=DMA((CH,)), p_r=DMA((CH,)),
-    i_s=DMA((2, 4)), i_r=DMA((2, 4)),
-    s1_s=DMA((C, 2, 4)), s1_r=DMA((C, 2, 4)),
-    s2_s=DMA((C, 3)), s2_r=DMA((C, 4)),
-    t1_s=DMA((C, 4)), t1_r=DMA((C, 2, 2)),
-    t2_s=DMA((C, 2, 4)), t2_r=DMA((C, 2, 4)),
-    v_s=DMA((C, CH)), v_r=DMA((C, CH)),
+    y_s=DMA((C,)), y_r=DMA((C, 2)),
+    p_s=DMA((1,)), p_r=DMA((1,)),
+    i_s=DMA((2,)), i_r=DMA((2,)),
+    s1_s=DMA((C, 2)), s1_r=DMA((C, 2)),
+    s2_s=DMA((C,)), s2_r=DMA((C,)),
+    t1_s=DMA((C,)), t1_r=DMA((C,)),
+    t2_s=DMA((C, 2)), t2_r=DMA((C, 2)),
+    v_s=DMA((C,)), v_r=DMA((C, 2)),
 )
 CHUNKED = dict(
     y_send=(CH, None, W),
@@ -70,9 +70,10 @@
 TN = ((0,), (0,))
 
 ORDER = [
-    "solved", "U0", "U1", "D0", "U2", "D1", "P0", "U3", "D2", "P1",
-    "K0", "D3", "P2", "K1", "gains", "R0", "P3", "parent", "K2", "F0",
-    "R1", "K3", "R2", "F1", "R3", "F2", "F3",
+    "solved", "U0", "U1", "D0", "D1", "P0", "U2", "P1", "K0", "U3",
+    "D2", "K1", "R0", "U4", "U5", "D3", "P2", "R1", "D4", "D5",
+    "P3", "K2", "P4", "gains", "P5", "parent", "K3", "F0", "F1", "R2",
+    "K4", "K5", "R3", "F2", "R4", "R5", "sent", "F3", "F4", "F5",
 ]
 
 
@@ -169,17 +170,8 @@
     t_self = own_pos // 2
     first_pos = (x, y)
 
-    def partner(j):
-        m = j // 2
-        step = jnp.where(m == 0, 2, jnp.where(m == 1, 1, jnp.where(m == 2, 3, 0)))
-        return ((z + step) % 4) * 2 + (core + j + m // 3) % 2
-
-    def each(first, last, action, unroll=1):
-        def one(j, carry):
-            action(j)
-            return carry
-
-        lax.fori_loop(first, last, one, 0, unroll=unroll)
+    partners = [((z + step) % 4) * 2 + (core + d) % 2 for step, d in ((2, 0), (2, 1), (1, 0), (1, 1), (3, 0), (3, 1), (0, 1), (0, 0))]
+    far, near = partners[:2], partners[2:7]
 
     def first_dev(f, a):
         return (r, a * 4 + y) if f == 0 else (r, x * 4 + a)
@@ -196,7 +188,8 @@
         )
 
     barrier = pltpu.get_barrier_semaphore()
-    each(0, 7, lambda j: pl.semaphore_signal(barrier, inc=1, device_id=(partner(j), q), device_id_type=MESH))
+    for k in partners[:7]:
+        pl.semaphore_signal(barrier, inc=1, device_id=(k, q), device_id_type=MESH)
     for f in range(2):
         for d in range(1, 4):
             pl.semaphore_signal(barrier, inc=1, device_id=first_dev(f, (first_pos[f] + d) % 4), device_id_type=MESH)
@@ -207,11 +200,9 @@
             pltpu.make_async_copy(rhs_hbm.at[k], rhs.at[k], load_sem.at[1, k]),
         )
 
-    def start_load(j):
-        for copy in load(partner(j)):
+    for k in partners:
+        for copy in load(k):
             copy.start()
-
-    each(0, 8, start_load)
     panel_load = pltpu.make_async_copy(panels_hbm, panels, load_sem.at[2, 0])
     rows_load = pltpu.make_async_copy(rows_hbm, rows, load_sem.at[2, 1])
     pinv_load = pltpu.make_async_copy(pinv_hbm, pinv, load_sem.at[2, 2])
@@ -219,11 +210,16 @@
     for copy in (rows_load, panel_load, pinv_load, prhs_load):
         copy.start()
 
-    def y_copy(c, k):
-        return remote(y_send[c].at[k], y_in[c].at[r], y_s.at[c, k], y_r.at[c, r], (k, q))
-
-    def y_wait(c, s):
-        return remote(y_send[c].at[s], y_in[c].at[s], y_s.at[c, s], y_r.at[c, s], (s, q))
+    def group(j):
+        return 0 if j < 2 else 1
+
+    def y_start(c, j):
+        k = partners[j]
+        remote(y_send[c].at[k], y_in[c].at[r], y_s.at[c], y_r.at[c, group(j)], (k, q)).start()
+
+    def y_wait(c, g):
+        blocks = y_in[c].at[pl.ds(0, (2, 5)[g])]
+        remote(blocks, blocks, y_s.at[c], y_r.at[c, g], (far[0], q)).wait_recv()
 
     def forward(k):
         for copy in load(k):
@@ -232,20 +228,19 @@
         for c in range(C):
             y_send[c][k] = value[STARTS[c]:STARTS[c] + WIDTHS[c]]
 
-    def forward_step(j):
-        forward(partner(j))
-        y_copy(0, partner(j)).start()
-
-    forward(partner(0))
+    forward(partners[0])
     pl.semaphore_wait(barrier, 13)
-    y_copy(0, partner(0)).start()
-    each(1, 7, forward_step)
+    y_start(0, 0)
+    for j in range(1, 7):
+        forward(partners[j])
+        y_start(0, j)
     forward(r)
     for c in range(C):
         y_in[c][r] = y_send[c][r]
 
     def y_follow(c):
-        each(0, 7, lambda j: y_copy(c, partner(j)).start())
+        for j in range(7):
+            y_start(c, j)
 
     def parent_of(f, a, t):
         if f == 0:
@@ -253,10 +248,11 @@
         return ((a + core + 1) % 2 + 2 * t) * 4 + a
 
     def rows_copy(f, a):
-        return remote(rows_send.at[f, a], rows_in.at[f, first_pos[f]], i_s.at[f, a], i_r.at[f, first_pos[f]], first_dev(f, a))
-
-    def rows_wait(f, a):
-        return remote(rows_send.at[f, a], rows_in.at[f, a], i_s.at[f, a], i_r.at[f, a], first_dev(f, a))
+        return remote(rows_send.at[f, a], rows_in.at[f, first_pos[f]], i_s.at[f], i_r.at[f], first_dev(f, a))
+
+    def rows_wait(f):
+        blocks = rows_in.at[f, pl.ds(0, 3)]
+        return remote(blocks, blocks, i_s.at[f], i_r.at[f], first_dev(f, (first_pos[f] + 1) % 4))
 
     def send_rows():
         rows_load.wait()
@@ -292,27 +288,29 @@
     def make_one_hot():
         places = lax.broadcasted_iota(jnp.int32, (W, R), 0)
         for f in range(2):
-            for d in range(1, 4):
-                rows_wait(f, (first_pos[f] + d) % 4).wait_recv()
+            rows_wait(f).wait_recv()
             for a in range(4):
                 for t in range(2):
                     matrix = jnp.where(places == rows_in[f, a, t:t + 1, :], 1.0, 0.0)
                     one_hot[f, t, :, a * R:(a + 1) * R] = matrix.astype(BF16)
 
     def first_copy(c, f, a):
-        return remote(first_send[c].at[f, a], first_in[c].at[f, first_pos[f]], s1_s.at[c, f, a], s1_r.at[c, f, first_pos[f]], first_dev(f, a))
-
-    def first_wait(c, f, a):
-        return remote(first_send[c].at[f, a], first_in[c].at[f, a], s1_s.at[c, f, a], s1_r.at[c, f, a], first_dev(f, a))
+        return remote(first_send[c].at[f, a], first_in[c].at[f, first_pos[f]], s1_s.at[c, f], s1_r.at[c, f], first_dev(f, a))
+
+    def first_wait(c, f):
+        blocks = first_in[c].at[f, pl.ds(0, 3)]
+        return remote(blocks, blocks, s1_s.at[c, f], s1_r.at[c, f], first_dev(f, (first_pos[f] + 1) % 4))
 
     def step_update(c):
         def one(s):
             update[c][s] = streamed(y_in[c][s], panel_high[s], panel_low[s], NT)
 
-        each(0, 5, lambda j: y_wait(c, partner(6 - j)).wait_recv())
-        each(0, 6, lambda j: one(partner(7 - j)), 6)
-        each(0, 2, lambda j: y_wait(c, partner(j)).wait_recv())
-        each(0, 2, lambda j: one(partner(j)), 2)
+        y_wait(c, 1)
+        for s in partners[2:]:
+            one(s)
+        y_wait(c, 0)
+        for s in far:
+            one(s)
         for f in range(2):
             for a in range(4):
                 for t in range(2):
@@ -327,19 +325,19 @@
 
     def second_own(c):
         a = (own_pos + 2) % 4
-        return remote(dense[c].at[cls, 1 - t_self], second_in[c].at[own_pos], s2_s.at[c, 2], s2_r.at[c, own_pos], own_dev(a))
+        return remote(dense[c].at[cls, 1 - t_self], second_in[c].at[own_pos], s2_s.at[c], s2_r.at[c], own_dev(a))
 
     def second_other(c, t):
         a = (other_pos + 1) % 2 + 2 * t
-        return remote(dense[c].at[1 - cls, t], second_in[c].at[other_pos], s2_s.at[c, t], s2_r.at[c, other_pos], other_dev(a))
-
-    def second_wait(c, a):
-        return remote(dense[c].at[0, 0], second_in[c].at[a], s2_s.at[c, 0], s2_r.at[c, a], own_dev(a))
+        return remote(dense[c].at[1 - cls, t], second_in[c].at[other_pos], s2_s.at[c], s2_r.at[c], other_dev(a))
+
+    def second_wait(c):
+        blocks = second_in[c].at[pl.ds(0, 3)]
+        return remote(blocks, blocks, s2_s.at[c], s2_r.at[c], own_dev((own_pos + 1) % 4))
 
     def step_dense(c):
         for f in range(2):
-            for d in (1, 3, 2):
-                first_wait(c, f, (first_pos[f] + d) % 4).wait_recv()
+            first_wait(c, f).wait_recv()
             for t in range(2):
                 blocks = jnp.concatenate([first_in[c][f, a, t] for a in range(4)], axis=1)
                 dense[c][f, t] = chosen(blocks, one_hot[f, t], NT)
@@ -348,21 +346,17 @@
             second_other(c, t).start()
 
     def x_copy(c, d):
-        return remote(x_block[c].at[cls, t_self], x_block[c].at[cls, t_self], t1_s.at[c, d], t1_r.at[c, cls, t_self], own_dev((own_pos + d) % 4))
-
-    def x_wait_own(c):
-        return remote(x_block[c].at[cls, 1 - t_self], x_block[c].at[cls, 1 - t_self], t1_s.at[c, 1], t1_r.at[c, cls, 1 - t_self], own_dev((own_pos + 2) % 4))
-
-    def x_wait_other(c, t):
-        a = (other_pos + 1) % 2 + 2 * t
-        return remote(x_block[c].at[1 - cls, t], x_block[c].at[1 - cls, t], t1_s.at[c, 1], t1_r.at[c, 1 - cls, t], other_dev(a))
+        return remote(x_block[c].at[cls, t_self], x_block[c].at[cls, t_self], t1_s.at[c], t1_r.at[c], own_dev((own_pos + d) % 4))
+
+    def x_wait(c):
+        blocks = second_in[c].at[pl.ds(0, 3)]
+        return remote(blocks, blocks, t1_s.at[c], t1_r.at[c], own_dev((own_pos + 1) % 4))
 
     def step_parent(c):
         total = dense[c][cls, t_self]
+        second_wait(c).wait_recv()
         for d in (1, 3, 2):
-            a = (own_pos + d) % 4
-            second_wait(c, a).wait_recv()
-            total = total + second_in[c][a]
+            total = total + second_in[c][(own_pos + d) % 4]
         value = z_parent[STARTS[c]:STARTS[c] + WIDTHS[c]] - streamed(total, k_high[...], k_low[...])
         x_block[c][cls, t_self] = value
         for d in (2, 1, 3):
@@ -370,15 +364,14 @@
         x_all[STARTS[c]:STARTS[c] + WIDTHS[c]] = value
 
     def pick_copy(c, f, a):
-        return remote(pick_send[c].at[f, a], pick_in[c].at[f, first_pos[f]], t2_s.at[c, f, a], t2_r.at[c, f, first_pos[f]], first_dev(f, a))
-
-    def pick_wait(c, f, a):
-        return remote(pick_send[c].at[f, a], pick_in[c].at[f, a], t2_s.at[c, f, a], t2_r.at[c, f, a], first_dev(f, a))
+        return remote(pick_send[c].at[f, a], pick_in[c].at[f, first_pos[f]], t2_s.at[c, f], t2_r.at[c, f], first_dev(f, a))
+
+    def pick_wait(c, f):
+        blocks = pick_in[c].at[f, pl.ds(0, 3)]
+        return remote(blocks, blocks, t2_s.at[c, f], t2_r.at[c, f], first_dev(f, (first_pos[f] + 1) % 4))
 
     def step_pick(c):
-        for t in range(2):
-            x_wait_other(c, t).wait_recv()
-        x_wait_own(c).wait_recv()
+        x_wait(c).wait_recv()
         for f in range(2):
             for t in range(2):
                 picked = chosen(x_block[c][f, t], one_hot[f, t])
@@ -388,16 +381,13 @@
             for d in (2, 1, 3):
                 pick_copy(c, f, (first_pos[f] + d) % 4).start()
 
-    def v_copy(c, s):
-        return remote(v_send[c].at[s], v_in[c].at[r], v_s.at[c, s], v_r.at[c, r], (s, q))
-
-    def v_wait(c, s):
-        return remote(v_send[c].at[s], v_in[c].at[s], v_s.at[c, s], v_r.at[c, s], (s, q))
+    def v_wait(c, g):
+        blocks = v_in[c].at[pl.ds(0, (2, 5)[g])]
+        remote(blocks, blocks, v_s.at[c], v_r.at[c, g], (far[0], q)).wait_recv()
 
     def step_return(c):
         for f in range(2):
-            for d in (1, 3, 2):
-                pick_wait(c, f, (first_pos[f] + d) % 4).wait_recv()
+            pick_wait(c, f).wait_recv()
 
         def one(s):
             p = parent_ids[s]
@@ -407,41 +397,40 @@
             t = jnp.where(f == 0, y_p, x_p) // 2
             v_send[c][s] = pick_in[c][f, a, t]
 
-        def go(j):
-            s = partner(j)
+        for j in range(7):
+            s = partners[j]
             one(s)
-            v_copy(c, s).start()
-
-        each(0, 7, go)
+            remote(v_send[c].at[s], v_in[c].at[r], v_s.at[c], v_r.at[c, group(j)], (s, q)).start()
         one(r)
         v_in[c][r] = v_send[c][r]
 
-    def panel_copy(k):
-        return remote(panels.at[k], panel_in.at[r], p_s.at[k], p_r.at[r], (k, q))
-
-    def panel_wait(s):
-        return remote(panels.at[s], panel_in.at[s], p_s.at[s], p_r.at[s], (s, q))
-
     def send_panels():
-        each(0, 7, lambda j: panel_copy(partner(j)).start())
+        for k in partners[:7]:
+            remote(panels.at[k], panel_in.at[r], p_s.at[0], p_r.at[0], (k, q)).start()
         panel_in[r] = panels[r]
 
+    def panel_wait():
+        blocks = panel_in.at[pl.ds(0, 7)]
+        return remote(blocks, blocks, p_s.at[0], p_r.at[0], (far[0], q))
+
     def gains():
-        each(0, 7, lambda j: panel_wait(partner(6 - j)).wait_recv())
+        panel_wait().wait_recv()
 
         def one(s):
             high, low = split(product(panel_in[s], inverse[s]))
             gain_high[s] = high
             gain_low[s] = low
 
-        each(0, CH, one, 4)
+        for s in range(CH):
+            one(s)
 
     def solved():
         def one(k):
             value = jnp.concatenate([y_send[c][k] for c in range(C)], axis=0)
             z_child[k] = product(value, inverse[k])
 
-        each(0, CH, one, 4)
+        for k in range(CH):
+            one(k)
 
     def out_copy(h, k):
         return pltpu.make_async_copy(out_buf.at[k, :, pl.ds(h * R, R)], child_out.at[k, :, pl.ds(h * R, R)], out_sem.at[h, k])
@@ -461,16 +450,37 @@
                 out_buf[s, :, half * R:(half + 1) * R] = value.T
                 out_copy(half, s).start()
 
-        each(0, 5, lambda j: v_wait(c, partner(6 - j)).wait_recv())
-        each(0, 6, lambda j: one(partner(7 - j)), 6)
-        each(0, 2, lambda j: v_wait(c, partner(j)).wait_recv())
-        each(0, 2, lambda j: one(partner(j)), 2)
+        v_wait(c, 1)
+        for s in partners[2:]:
+            one(s)
+        v_wait(c, 0)
+        for s in far:
+            one(s)
 
     x_out = pltpu.make_async_copy(x_all, parent_out, out_sem.at[2, 0])
 
     def parent_result():
         x_all[...] = x_all[...].T
         x_out.start()
+
+    def v_sent(c):
+        blocks = v_in[c].at[pl.ds(0, 7)]
+        remote(blocks, blocks, v_s.at[c], v_r.at[c, 0], (far[0], q)).wait_send()
+
+    def sent():
+        panel_wait().wait_send()
+        for f in range(2):
+            rows_wait(f).wait_send()
+        for c in range(C):
+            blocks = y_in[c].at[pl.ds(0, 7)]
+            remote(blocks, blocks, y_s.at[c], y_r.at[c, 0], (far[0], q)).wait_send()
+            for f in range(2):
+                first_wait(c, f).wait_send()
+                pick_wait(c, f).wait_send()
+            second_wait(c).wait_send()
+            x_wait(c).wait_send()
+        for c in range(C - 1):
+            v_sent(c)
 
     steps = dict(U=step_update, D=step_dense, P=step_parent, K=step_pick, R=step_return, F=step_final)
     send_rows()
@@ -487,38 +497,31 @@
             gains()
         elif step == "parent":
             parent_result()
+        elif step == "sent":
+            sent()
         else:
             steps[step[0]](int(step[1:]))
 
-    def z_done(j):
-        k = partner(j)
-        panel_copy(k).wait_send()
-        for c in range(C):
-            y_copy(c, k).wait_send()
-        for c in range(C):
-            v_copy(c, k).wait_send()
-
-    each(0, 7, z_done)
-    for f in range(2):
-        for d in range(1, 4):
-            a = (first_pos[f] + d) % 4
-            rows_copy(f, a).wait_send()
-            for c in range(C):
-                first_copy(c, f, a).wait_send()
-                pick_copy(c, f, a).wait_send()
-    for c in range(C):
-        second_own(c).wait_send()
-        for t in range(2):
-            second_other(c, t).wait_send()
-        for d in range(1, 4):
-            x_copy(c, d).wait_send()
-
-    def out_done(k):
-        for h in range(2):
+    v_sent(C - 1)
+
+    for h in range(2):
+        for k in range(CH):
             out_copy(h, k).wait()
-
-    each(0, CH, out_done)
     x_out.wait()
+
+
+def hand_over(child, parent, child_out, parent_out, in_sems, out_sems, held, held_parent):
+    ins = [pltpu.make_async_copy(child.at[k], held.at[k], in_sems.at[k]) for k in range(CH)]
+    ins.append(pltpu.make_async_copy(parent, held_parent, in_sems.at[CH]))
+    outs = [pltpu.make_async_copy(held.at[k], child_out.at[k], out_sems.at[k]) for k in range(CH)]
+    outs.append(pltpu.make_async_copy(held_parent, parent_out, out_sems.at[CH]))
+    for copy in ins:
+        copy.start()
+    for first, second in zip(ins, outs):
+        first.wait()
+        second.start()
+    for copy in outs:
+        copy.wait()
 
 
 def body(child_inverse, child_rhs, panels, panel_parent, panel_rows, parent_inverse, parent_rhs):
@@ -535,6 +538,13 @@
         panel_parent.reshape(CH), child_inverse[0, 0], child_rhs[0, 0], panels[0, 0], panel_rows[0, 0],
         parent_inverse[0, 0], parent_rhs[0, 0],
     )
+    child, parent = pl.pallas_call(
+        hand_over,
+        out_shape=(jax.ShapeDtypeStruct((CH, W, W), F32), jax.ShapeDtypeStruct((W, W), F32)),
+        in_specs=[anywhere] * 2,
+        out_specs=(anywhere, anywhere),
+        scratch_shapes=[DMA((CH + 1,)), DMA((CH + 1,)), pltpu.VMEM((CH, W, W), F32), pltpu.VMEM((W, W), F32)],
+    )(child, parent)
     return child[None, None], parent[None, None]
 
 

time: 74.1 us -> 69.3 us (0.935)
  local copies, waits for them, and re-layouts: 3.79 us -> 0 us
  Pallas kernels: 69.5 us -> 68.5 us
    unnamed x4 -> x0, local copies, waits for them, and re-layouts: 3.79 us -> none
    pallas_call x1, Pallas kernels: 69.5 us -> 66 us  [body(): pl.pallas_call(kernel, out_shape=(jax.ShapeDtypeStruct((CH, W, W), F32),...]
    pallas_call x0 -> x1, Pallas kernels: none -> 2.5 us  [body(): pl.pallas_call(hand_over, out_shape=(jax.ShapeDtypeStruct((CH, W, W), F32...]
where the time goes in v4:
time: 69.3 us; the launch traced here: 69.1 us
  Pallas kernels  68.5 us (99%)
    pallas_call x1, Pallas kernels, body(): pl.pallas_call(kernel, out_shape=(jax.ShapeDtypeStruct((CH, W, W), F32),...  66 us
    pallas_call x1, Pallas kernels, body(): pl.pallas_call(hand_over, out_shape=(jax.ShapeDtypeStruct((CH, W, W), F32...  2.5 us

profile of v4, /device:TPU:1, one launch (start us, length us, event | category | flops | bytes accessed | tf_op | source)
XLA Modules:
  0.0 69.1 jit_solution(5772725419997028208)
XLA Ops:
  0.6 66.0 %shard_map.86 = (f32[8,256,256]{2,1,0:T(8,128)}, f32[256,256]{1,0:T(8,128)}) custom-call(s32[8]{0:T(128)} %bitcast.17, f32[8,256,256]{2,1,0:T(8,128)} %bitcast.9, f32[8,256,256]{2,1,0:T(8,128)} %bitcast.10, f32[8,128,256]{2,1,0:T(8,128)} %bitcast.12, s32[8,128]{1,0:T(8,128)} %bitcast.16, f32[256,256]{1,0:T(8,128)} %bitcast.13, f32[256,256]{1,0:T(8,128)} %bitcast.14), custom_call_target="tpu_custom_call" | custom-call | flops 4200000000 | bytes 8388608 | tf_op jit(solution)/shard_map/pallas_call | solution.py:529
  66.6 2.5 %shard_map.87 = (f32[8,256,256]{2,1,0:T(8,128)}, f32[256,256]{1,0:T(8,128)}) custom-call(f32[8,256,256]{2,1,0:T(8,128)} %get-tuple-element.6.child, f32[256,256]{1,0:T(8,128)} %get-tuple-element.7.parent), custom_call_target="tpu_custom_call" | custom-call | tf_op jit(solution)/shard_map/pallas_call | solution.py:541

commit v5 on v4

--- a/solution.py
+++ b/solution.py
@@ -33,12 +33,11 @@
     z_parent=pltpu.VMEM((W, W), F32),
     x_all=pltpu.VMEM((W, W), F32),
     panel_in=pltpu.VMEM((CH, R, W), F32),
-    gain_high=pltpu.VMEM((CH, R, W), BF16),
-    gain_low=pltpu.VMEM((CH, R, W), BF16),
+    gain_high=pltpu.VMEM((CH, W, R), BF16),
+    gain_low=pltpu.VMEM((CH, W, R), BF16),
+    v_in=pltpu.VMEM((CH, W, R), F32),
     z_child=pltpu.VMEM((CH, W, W), F32),
-    out_buf=pltpu.VMEM((CH, W, W), F32),
     load_sem=DMA((3, CH)),
-    out_sem=DMA((3, CH)),
     y_s=DMA((C,)), y_r=DMA((C, 2)),
     p_s=DMA((1,)), p_r=DMA((1,)),
     i_s=DMA((2,)), i_r=DMA((2,)),
@@ -60,7 +59,6 @@
     pick_send=(2, 4, 2, None, R),
     pick_in=(2, 4, 2, None, R),
     v_send=(CH, None, R),
-    v_in=(CH, None, R),
 )
 for name, shape in CHUNKED.items():
     for c in range(C):
@@ -72,8 +70,8 @@
 ORDER = [
     "solved", "U0", "U1", "D0", "D1", "P0", "U2", "P1", "K0", "U3",
     "D2", "K1", "R0", "U4", "U5", "D3", "P2", "R1", "D4", "D5",
-    "P3", "K2", "P4", "gains", "P5", "parent", "K3", "F0", "F1", "R2",
-    "K4", "K5", "R3", "F2", "R4", "R5", "sent", "F3", "F4", "F5",
+    "P3", "K2", "P4", "gains", "P5", "parent", "K3", "R2", "K4", "K5",
+    "R3", "F2", "R4", "R5", "sent", "F5",
 ]
 
 
@@ -128,9 +126,7 @@
     gain_high = ref["gain_high"]
     gain_low = ref["gain_low"]
     z_child = ref["z_child"]
-    out_buf = ref["out_buf"]
     load_sem = ref["load_sem"]
-    out_sem = ref["out_sem"]
     y_s = ref["y_s"]
     y_r = ref["y_r"]
     p_s = ref["p_s"]
@@ -158,7 +154,7 @@
     pick_send = [ref["pick_send" + str(c)] for c in range(C)]
     pick_in = [ref["pick_in" + str(c)] for c in range(C)]
     v_send = [ref["v_send" + str(c)] for c in range(C)]
-    v_in = [ref["v_in" + str(c)] for c in range(C)]
+    v_in = ref["v_in"]
 
     r = lax.axis_index("prow")
     q = lax.axis_index("pcol")
@@ -382,7 +378,7 @@
                 pick_copy(c, f, (first_pos[f] + d) % 4).start()
 
     def v_wait(c, g):
-        blocks = v_in[c].at[pl.ds(0, (2, 5)[g])]
+        blocks = v_in.at[pl.ds(0, (2, 5)[g]), pl.ds(0, WIDTHS[c])]
         remote(blocks, blocks, v_s.at[c], v_r.at[c, g], (far[0], q)).wait_recv()
 
     def step_return(c):
@@ -400,9 +396,9 @@
         for j in range(7):
             s = partners[j]
             one(s)
-            remote(v_send[c].at[s], v_in[c].at[r], v_s.at[c], v_r.at[c, group(j)], (s, q)).start()
+            remote(v_send[c].at[s], v_in.at[r, pl.ds(STARTS[c], WIDTHS[c])], v_s.at[c], v_r.at[c, group(j)], (s, q)).start()
         one(r)
-        v_in[c][r] = v_send[c][r]
+        v_in[r, STARTS[c]:STARTS[c] + WIDTHS[c]] = v_send[c][r]
 
     def send_panels():
         for k in partners[:7]:
@@ -417,7 +413,7 @@
         panel_wait().wait_recv()
 
         def one(s):
-            high, low = split(product(panel_in[s], inverse[s]))
+            high, low = split(product(panel_in[s], inverse[s]).T)
             gain_high[s] = high
             gain_low[s] = low
 
@@ -427,44 +423,35 @@
     def solved():
         def one(k):
             value = jnp.concatenate([y_send[c][k] for c in range(C)], axis=0)
-            z_child[k] = product(value, inverse[k])
+            z_child[k] = product(value, inverse[k]).T
 
         for k in range(CH):
             one(k)
 
-    def out_copy(h, k):
-        return pltpu.make_async_copy(out_buf.at[k, :, pl.ds(h * R, R)], child_out.at[k, :, pl.ds(h * R, R)], out_sem.at[h, k])
-
     def step_final(c):
-        start = STARTS[c]
-        end = start + WIDTHS[c]
-        half = start // R
+        h = STARTS[c] // R
+        chunks = [n for n in range(C) if STARTS[n] // R == h]
 
         def one(s):
-            value = z_child[s, start:end] - streamed(v_in[c][s], gain_high[s], gain_low[s])
-            if end % R:
-                z_child[s, start:end] = value
-            else:
-                if start % R:
-                    value = jnp.concatenate([z_child[s, half * R:start], value], axis=0)
-                out_buf[s, :, half * R:(half + 1) * R] = value.T
-                out_copy(half, s).start()
-
-        v_wait(c, 1)
+            v_high, v_low = split(v_in[s, h * R:(h + 1) * R])
+            g_high = gain_high[s]
+            term = dot(g_high, v_high, NT) + (dot(g_high, v_low, NT) + dot(gain_low[s], v_high, NT))
+            child_out[s, :, h * R:(h + 1) * R] = z_child[s, :, h * R:(h + 1) * R] - term
+
+        for n in chunks:
+            v_wait(n, 1)
         for s in partners[2:]:
             one(s)
-        v_wait(c, 0)
+        for n in chunks:
+            v_wait(n, 0)
         for s in far:
             one(s)
 
-    x_out = pltpu.make_async_copy(x_all, parent_out, out_sem.at[2, 0])
-
     def parent_result():
-        x_all[...] = x_all[...].T
-        x_out.start()
+        parent_out[...] = x_all[...].T
 
     def v_sent(c):
-        blocks = v_in[c].at[pl.ds(0, 7)]
+        blocks = v_in.at[pl.ds(0, 7), pl.ds(0, WIDTHS[c])]
         remote(blocks, blocks, v_s.at[c], v_r.at[c, 0], (far[0], q)).wait_send()
 
     def sent():
@@ -504,33 +491,15 @@
 
     v_sent(C - 1)
 
-    for h in range(2):
-        for k in range(CH):
-            out_copy(h, k).wait()
-    x_out.wait()
-
-
-def hand_over(child, parent, child_out, parent_out, in_sems, out_sems, held, held_parent):
-    ins = [pltpu.make_async_copy(child.at[k], held.at[k], in_sems.at[k]) for k in range(CH)]
-    ins.append(pltpu.make_async_copy(parent, held_parent, in_sems.at[CH]))
-    outs = [pltpu.make_async_copy(held.at[k], child_out.at[k], out_sems.at[k]) for k in range(CH)]
-    outs.append(pltpu.make_async_copy(held_parent, parent_out, out_sems.at[CH]))
-    for copy in ins:
-        copy.start()
-    for first, second in zip(ins, outs):
-        first.wait()
-        second.start()
-    for copy in outs:
-        copy.wait()
-
 
 def body(child_inverse, child_rhs, panels, panel_parent, panel_rows, parent_inverse, parent_rhs):
     anywhere = pl.BlockSpec(memory_space=pl.ANY)
+    vmem = pl.BlockSpec(memory_space=pltpu.VMEM)
     child, parent = pl.pallas_call(
         kernel,
-        out_shape=(jax.ShapeDtypeStruct((CH, W, W), F32), jax.ShapeDtypeStruct((W, W), F32)),
+        out_shape=(pltpu.VMEM((CH, W, W), F32), pltpu.VMEM((W, W), F32)),
         in_specs=[pl.BlockSpec(memory_space=pltpu.SMEM)] + [anywhere] * 6,
-        out_specs=(anywhere, anywhere),
+        out_specs=(vmem, vmem),
         scratch_shapes=list(SCRATCH.values()),
         compiler_params=pltpu.CompilerParams(collective_id=0, has_side_effects=True, vmem_limit_bytes=56 << 20),
         cost_estimate=pl.CostEstimate(flops=2 * 2100 * 10**6, bytes_accessed=8 << 20, transcendentals=0),
@@ -538,13 +507,6 @@
         panel_parent.reshape(CH), child_inverse[0, 0], child_rhs[0, 0], panels[0, 0], panel_rows[0, 0],
         parent_inverse[0, 0], parent_rhs[0, 0],
     )
-    child, parent = pl.pallas_call(
-        hand_over,
-        out_shape=(jax.ShapeDtypeStruct((CH, W, W), F32), jax.ShapeDtypeStruct((W, W), F32)),
-        in_specs=[anywhere] * 2,
-        out_specs=(anywhere, anywhere),
-        scratch_shapes=[DMA((CH + 1,)), DMA((CH + 1,)), pltpu.VMEM((CH, W, W), F32), pltpu.VMEM((W, W), F32)],
-    )(child, parent)
     return child[None, None], parent[None, None]
 
 

time: 69.3 us -> 68.1 us (0.983)
  Pallas kernels: 68.5 us -> 65.3 us
  local copies, waits for them, and re-layouts: 0 us -> 2.02 us
    pallas_call x2 -> x1, Pallas kernels: 68.5 us -> 65.3 us  [body(): pl.pallas_call(kernel, out_shape=(pltpu.VMEM((CH, W, W), F32), pltpu.VMEM...]
    unnamed x0 -> x2, local copies, waits for them, and re-layouts: none -> 2.02 us
where the time goes in v5:
time: 68.1 us; the launch traced here: 68 us
  Pallas kernels  65.3 us (96%)
  local copies, waits for them, and re-layouts  2.02 us (3%)
    pallas_call x1, Pallas kernels, body(): pl.pallas_call(kernel, out_shape=(pltpu.VMEM((CH, W, W), F32), pltpu.VMEM...  65.3 us
    unnamed x2, local copies, waits for them, and re-layouts  2.02 us

profile of v5, /device:TPU:1, one launch (start us, length us, event | category | flops | bytes accessed | tf_op | source)
XLA Modules:
  0.0 68.0 jit_solution(17571693852053283630)
XLA Ops:
  0.6 65.3 %shard_map.86 = (f32[8,256,256]{2,1,0:T(8,128)S(1)}, f32[256,256]{1,0:T(8,128)S(1)}) custom-call(s32[8]{0:T(128)} %bitcast.17, f32[8,256,256]{2,1,0:T(8,128)} %bitcast.11, f32[8,256,256]{2,1,0:T(8,128)} %bitcast.12, f32[8,128,256]{2,1,0:T(8,128)} %bitcast.13, s32[8,128]{1,0:T(8,128)} %bitcast.16, f32[256,256]{1,0:T(8,128)} %bitcast.14, f32[256,256]{1,0:T(8,128)} %bitcast.15), custom_call_target="tpu_custom_call" | custom-call | flops 4200000000 | bytes 8388608 | tf_op jit(solution)/shard_map/pallas_call | solution.py:498
  65.9 1.3 %copy.11 = f32[1,1,8,256,256]{4,3,2,1,0:T(8,128)} copy(f32[1,1,8,256,256]{4,3,2,1,0:T(8,128)S(1)} %bitcast.9) | data formatting | bytes 4194304
  67.3 0.7 %copy.12 = f32[1,1,256,256]{3,2,1,0:T(8,128)} copy(f32[1,1,256,256]{3,2,1,0:T(8,128)S(1)} %bitcast.10) | data formatting | bytes 524288
